TPU v7x, 32 devices: a whole 2x2x4 slice. The times are simulated.
32 devices in a mesh: sec: 2 (over x), batch: 16 (over z, y, core), head: 1.
Axes of the slice: x: 2, y: 2, z: 4, core: 2. Of those that a mesh axis runs over, the one named last changes fastest.
Arguments:
- hidden_in: bfloat16 [512, 7168], P('batch'), may hold values from -6 to 6
- queries: bfloat16 [512, 128, 576], P('batch', ('sec', 'head')), may hold values from -8 to 8
- latent_cache: bfloat16 [512, 192, 576], P('batch'), may hold values from -8 to 8
- new_latent: bfloat16 [512, 576], P('batch'), may hold values from -8 to 8
- cache_lengths: int32 [512], P('batch'), may hold values from 1 to 192, 49152 in all
- value_up: bfloat16 [128, 512, 128], P(('sec', 'head')), may hold values from -0.25 to 0.25
- out_proj: bfloat16 [16384, 7168], P(('sec', 'head'), 'batch'), may hold values from -0.046875 to 0.046875
- norm_gain: float32 [7168], replicated, may hold values from 0.1 to 1.9
- router: bfloat16 [7168, 16], replicated, may hold values from -0.03125 to 0.03125
- expert_ids: int32 [512, 8], P('batch'), may hold values from 0 to 15, all different within a row; in each aligned block of 32 rows (0 to 31, 32 to 63, ...) at most 32 rows name the same one
- w_gate_up: bfloat16 [16, 7168, 2, 1024], P('batch', None, None, ('sec', 'head')), may hold values from -0.0625 to 0.0625
- w_down: bfloat16 [16, 1024, 7168], P('batch', ('sec', 'head')), may hold values from -0.1875 to 0.1875
Outputs:
- mixed_out: bfloat16 [512, 7168], P('batch', ('sec', 'head'))
Inputs may be any that keep to these rules, and one draw needn't show every extreme that they name: `expert_ids`: each row names 8 different experts. Among the 32 rows of one index of batch (aligned blocks) no expert is named by more than 32 rows, a bound that some block reaches. `cache_lengths`: the lengths of all rows add up to 49152, and one row has exactly 192.
All inputs are finite; a program needn't handle non-finite values. No bound on the sum of `cache_lengths` on one device may be relied on, other than what follows from the above.
Results may differ from a plain program's by a relative error of at most 0.007.
Values may be sent and summed in bfloat16 or wider, within the bound.
No kernel may reach another device: no remote copies, remote signals or barrier semaphores. Data moves between devices by JAX's collectives and lax.ppermute only.
A program may use at most 128 MiB of HBM per device.

v0:
```python
import functools

import jax
import jax.numpy as jnp
from jax import lax
from jax.experimental import pallas as pl
from jax.experimental.pallas import tpu as pltpu
from jax.sharding import Mesh, PartitionSpec as P

QKD = 192
TOP = 8

norm_epsilon = 1e-06
route_scale = 2.5

GROUP = ("sec", "head")
SWAP = [(0, 1), (1, 0)]
STREAMS = 2
VMEM = 56 * 1024 * 1024
NT = (((1,), (1,)), ((), ()))
ANY = pl.BlockSpec(memory_space=pl.ANY)
IN_HBM = pl.BlockSpec(memory_space=pltpu.HBM)
IN_VMEM = pl.BlockSpec(memory_space=pltpu.VMEM)
IN_SMEM = pl.BlockSpec(memory_space=pltpu.SMEM)


def attend(queries, latent_cache, new_latent, cache_lengths, value_up):
    row_count = queries.shape[0]
    latent_width = value_up.shape[1]
    cache_depth = latent_cache.shape[1]
    score_scale = QKD ** (-0.5)
    scores = (
        jnp.einsum("thk,tjk->thj", queries, latent_cache, preferred_element_type=jnp.float32)
        * score_scale
    )
    own_score = (
        jnp.einsum("thk,tk->th", queries, new_latent, preferred_element_type=jnp.float32)
        * score_scale
    )
    positions = lax.broadcasted_iota(jnp.int32, (1, 1, cache_depth), 2)
    in_cache = positions < cache_lengths[:, None, None]
    scores = jnp.where(in_cache, scores, -jnp.inf)
    top_score = jnp.maximum(jnp.max(scores, axis=2), own_score)
    cache_exp = jnp.exp(scores - top_score[:, :, None])
    own_exp = jnp.exp(own_score - top_score)
    softmax_sum = jnp.sum(cache_exp, axis=2) + own_exp
    cache_weights = (cache_exp / softmax_sum[:, :, None]).astype(jnp.bfloat16)
    own_weights = (own_exp / softmax_sum).astype(jnp.bfloat16)
    latent_out = jnp.einsum(
        "thj,tjc->thc",
        cache_weights,
        latent_cache[:, :, :latent_width],
        preferred_element_type=jnp.float32,
    )
    latent_out = latent_out + own_weights.astype(jnp.float32)[:, :, None] * new_latent[
        :, None, :latent_width
    ].astype(jnp.float32)
    latent_out = latent_out.astype(jnp.bfloat16)
    head_out = jnp.einsum(
        "thc,hcd->thd", latent_out, value_up, preferred_element_type=jnp.float32
    ).astype(jnp.bfloat16)
    return head_out.reshape(row_count, -1)


def place_of(chip, chips):
    return jnp.where(chip % 2 == 0, chip // 2, chips - 1 - chip // 2)


def chip_at(place, chips):
    place = place % chips
    return jnp.where(place < chips // 2, 2 * place, 2 * (chips - 1 - place) + 1)


def ring_step(block):
    chips = lax.axis_size("chip")
    ring = list(range(0, chips, 2)) + list(range(chips - 1, 0, -2))
    pairs = []
    for i in range(chips):
        here, there = ring[i], ring[(i + 1) % chips]
        pairs += [(2 * here, 2 * there), (2 * there + 1, 2 * here + 1)]
    return lax.ppermute(block, ("chip", "core"), pairs)


def swap_cores(block):
    return lax.ppermute(block, "core", SWAP)


def by_core(core, first, second):
    return jnp.where(core == 0, first, second), jnp.where(core == 0, second, first)


def ring_gather(blocks, between):
    chips = lax.axis_size("chip")
    core = lax.axis_index("core")
    pieces, moving = [[block] for block in blocks], list(blocks)
    for i in range(chips // 2 - 1):
        for s in range(STREAMS):
            moving[s] = ring_step(between(s, i, moving[s], pieces))
            if i < chips // 2 - 2:
                pieces[s] += [moving[s], swap_cores(moving[s])]
    moving = between(STREAMS - 1, None, moving, pieces)
    for s in range(STREAMS):
        pieces[s] += [moving[s], swap_cores(moving[s])]
    last = between(None, chips // 2 - 1, jnp.where(core == 0, moving[0], moving[1]), pieces)
    last = between(None, None, ring_step(last), pieces)
    for s, piece in enumerate(by_core(core, last, swap_cores(last))):
        pieces[s].append(piece)
    return pieces


def ring_order():
    chips = lax.axis_size("chip")
    place = place_of(lax.axis_index("chip"), chips)
    sign = 2 * lax.axis_index("core") - 1
    places = [place]
    for d in range(1, chips // 2):
        places += [place + sign * d, place - sign * d]
    places.append(place + chips // 2)
    return [chip_at(p, chips) for p in places]


def plus(a, b):
    return a.astype(jnp.float32) + b.astype(jnp.float32)


def reduce_rows():
    chips = lax.axis_size("chip")
    core = lax.axis_index("core")
    chip = lax.axis_index("chip")
    place = place_of(chip, chips)
    far = 2 * chip_at(place + chips // 2, chips)

    def way(side, sign):
        blocks = []
        for d in range(chips // 2 - 1, 0, -1):
            at = 2 * chip_at(place + sign * d, chips)
            blocks += [at, at + 1]
        return [far + side] + blocks[:2], blocks[2:] + [2 * chip + side]

    sign = 1 - 2 * core
    keep, give = way(core, sign), way(1 - core, -sign)
    return keep[0] + give[0], keep[1] + give[1]


def ring_reduce(keep, got, between):
    core = lax.axis_index("core")
    group, groups = lax.axis_index(GROUP), lax.axis_size(GROUP)
    rows = keep[0].shape[0] // 3

    def cut(at, size, s):
        def one(parts):
            part, start = (parts[0], at) if at < 3 * rows else (parts[1], at - 3 * rows)
            half = part.shape[1] // STREAMS
            first = (group + 1 + s) % STREAMS if groups == STREAMS else s
            return lax.dynamic_slice(part, (start, first * half), (size, half))

        return plus(one(keep), one(got))

    moving = [ring_step(cut(0, rows, s).astype(jnp.bfloat16)) for s in range(STREAMS)]
    moving = [
        jnp.concatenate([jnp.where(core == 0, m, 0), jnp.where(core == 0, 0, m)], axis=0)
        for m in moving
    ]
    at, ahead, ready = rows, None, None
    total = 3 * rows + keep[1].shape[0]
    while at < total - rows:
        for s in range(STREAMS):
            if ahead is not None:
                moving[s], _ = lax.optimization_barrier((moving[s], ahead))
            ahead = plus(cut(at, 2 * rows, s), moving[s]).astype(jnp.bfloat16)
            if at == rows and s == STREAMS - 1:
                ready = between(ahead)
            if at > rows and s == STREAMS - 1:
                ahead, ready = lax.optimization_barrier((ahead, ready))
            moving[s] = ring_step(ahead)
        at += 2 * rows
    sums = []
    for s in range(STREAMS):
        if sums:
            moving[s], _ = lax.optimization_barrier((moving[s], sums[0]))
        mine, theirs = by_core(core, moving[s][:rows], moving[s][rows:])
        added = plus(cut(at, rows, s), plus(mine, swap_cores(theirs)))
        if groups == STREAMS and s == 0:
            added = lax.ppermute(added.astype(jnp.bfloat16), "sec", SWAP)
        sums.append(added)
    return sums, ready


def stream(count, ahead, copy):
    for k in range(min(ahead, count)):
        copy(k).start()

    def ready(k):
        copy(k).wait()

        @pl.when(k + ahead < count)
        def _():
            copy(k + ahead).start()

    return ready


def project_kernel(steps, ahead, count, weight, *refs):
    pieces, (out, rows, held, turned, piece_sems, weight_sems) = refs[:-6], refs[-6:]
    few = out.shape[0] <= 128
    depth = held.shape[2]
    block, half = pieces[0].shape
    copies = []
    for i, piece in enumerate(pieces):
        at, s = i % count, i // count
        target = rows.at[pl.ds(at * block, block), pl.ds(s * half, half)]
        copies.append(pltpu.make_async_copy(piece, target, piece_sems.at[i]))
    for copy in copies:
        copy.start()

    def weight_copy(k):
        columns = pl.ds(pl.multiple_of(k * depth, depth), depth)
        slot = k % (ahead + 1)
        return pltpu.make_async_copy(weight.at[:, columns], held.at[slot], weight_sems.at[slot])

    ready = stream(steps, ahead, weight_copy)
    for copy in copies:
        copy.wait()
    total = turned if few else out
    total[...] = jnp.zeros_like(total)

    @pl.loop(0, steps)
    def _(k):
        ready(k)
        columns = pl.ds(pl.multiple_of(k * depth, depth), depth)
        left, right = rows[:, columns], held[k % (ahead + 1)]
        if few:
            left, right = right, left
        total[...] += lax.dot_general(left, right, NT, preferred_element_type=jnp.float32)

    if few:
        out[...] = turned[...].T


def project(pieces, weight, ahead, grant):
    count = len(pieces[0])
    rows, half = pieces[0][0].shape
    depth = STREAMS * half
    columns = weight.shape[0]
    steps = 8
    total = count * rows
    return pl.pallas_call(
        functools.partial(project_kernel, steps, ahead, count),
        out_shape=jax.ShapeDtypeStruct((total, columns), jnp.float32),
        in_specs=[ANY] * (1 + STREAMS * count),
        out_specs=IN_VMEM,
        scratch_shapes=[
            pltpu.VMEM((total, depth), jnp.bfloat16),
            pltpu.VMEM((ahead + 1, columns, depth // steps), jnp.bfloat16),
            pltpu.VMEM((columns, total) if total <= 128 else (8, 128), jnp.float32),
            pltpu.SemaphoreType.DMA((STREAMS * count,)),
            pltpu.SemaphoreType.DMA((ahead + 1,)),
        ],
        compiler_params=pltpu.CompilerParams(vmem_limit_bytes=grant),
        cost_estimate=pl.CostEstimate(
            flops=2 * total * depth * columns,
            bytes_accessed=2 * depth * (total + columns) + 4 * total * columns,
            transcendentals=0,
        ),
    )(weight, *[piece for part in pieces for piece in part])


def finish_kernel(count, meta, arrived, gain, router, *refs):
    parts, got, (out, stats) = refs[:count], refs[count : 2 * count], refs[2 * count :]
    chips, rows, columns = out.shape
    names = router.shape[0]
    core = meta[chips] % 2
    i = 0
    for part, other in zip(parts, got):
        for j in range(part.shape[0] // rows):
            at = meta[i]
            block = part[j * rows : (j + 1) * rows, :] + other[j * rows : (j + 1) * rows, :].astype(jnp.float32)
            hidden = arrived[at].astype(jnp.float32)
            hidden = jnp.where(core == 0, hidden[:, :columns], hidden[:, columns : 2 * columns])
            block = hidden + block
            scaled = (block * gain[...]).astype(jnp.bfloat16)
            out[at] = scaled
            stats[at, :, :names] = lax.dot_general(
                scaled, router[...], NT, preferred_element_type=jnp.float32
            )
            stats[at, :, names : names + 1] = jnp.sum(block * block, axis=1, keepdims=True)
            i += 1


def finish(meta, parts, got, arrived, gain, router):
    columns = parts[0].shape[1]
    chips, rows, _ = arrived.shape
    return pl.pallas_call(
        functools.partial(finish_kernel, len(parts)),
        out_shape=(
            jax.ShapeDtypeStruct((chips, rows, columns), jnp.bfloat16),
            jax.ShapeDtypeStruct((chips, rows, router.shape[0] + 1), jnp.float32),
        ),
        in_specs=[IN_SMEM] + [IN_VMEM] * (3 + 2 * len(parts)),
        out_specs=(IN_VMEM, IN_VMEM),
        compiler_params=pltpu.CompilerParams(vmem_limit_bytes=16 * 1024 * 1024),
    )(meta, arrived, gain, router, *parts, *got)


def own_kernel(count, meta, *refs):
    pieces, (out, sems) = refs[:-2], refs[-2:]
    chips, share, _ = out.shape
    half = chips * share
    place = meta[chips]
    for s in range(STREAMS):

        @pl.when(place * share // half == s)
        def _():
            at = pl.ds(pl.multiple_of(place * share - s * half, share), share)
            copies = [
                pltpu.make_async_copy(pieces[s * count + i].at[at, :], out.at[meta[i]], sems.at[i])
                for i in range(count)
            ]
            for copy in copies:
                copy.start()
            for copy in copies:
                copy.wait()


def own_residual(meta, pieces, share):
    chips = len(pieces[0])
    depth = pieces[0][0].shape[1]
    return pl.pallas_call(
        functools.partial(own_kernel, chips),
        out_shape=jax.ShapeDtypeStruct((chips, share, depth), jnp.bfloat16),
        in_specs=[IN_SMEM] + [ANY] * (STREAMS * chips),
        out_specs=IN_VMEM,
        scratch_shapes=[pltpu.SemaphoreType.DMA((chips,))],
        compiler_params=pltpu.CompilerParams(vmem_limit_bytes=VMEM),
    )(meta, *[piece for part in pieces for piece in part])


def piece_starts(pieces, count, held, sems):
    half = held.shape[1] // STREAMS
    depth = pieces[0].shape[1]
    for i in range(count):
        for s in range(STREAMS):
            at = i // (held.shape[2] // depth)
            target = held.at[at, pl.ds(s * half, half), :]
            if held.shape[2] != depth:
                target = target.at[:, pl.ds(i % 2 * depth, depth)]
            source = pieces[s * count + i].at[pl.ds(0, half), :]
            pltpu.make_async_copy(source, target, sems.at[i]).start()


def add_products(count, depth, held, weight, total, piece_sems, weight_sems):
    per = held.shape[2] // depth

    def ready(k, at):
        block = held.at[k] if per == 1 else held.at[k, :, pl.ds(at * depth, depth)]
        wait_for(block, piece_sems.at[per * k + at])
        wait_for(weight.at[k, pl.ds(at * depth, depth), :], weight_sems.at[per * k + at])

    def add(k, deep):
        for at in range(0, total.shape[1], 256):
            total[:, at : at + 256] += jnp.dot(
                held[k, :, :deep],
                weight[k, :deep, at : at + 256],
                preferred_element_type=jnp.float32,
            )

    total[...] = jnp.zeros_like(total)

    @pl.loop(0, count // per)
    def _(k):
        for at in range(per):
            ready(k, at)
        add(k, per * depth)

    if count % per:
        ready(count // per, 0)
        add(count // per, depth)


def weight_start(at, gate_up, depth, per, target, sem):
    for p, part in enumerate(gate_up):

        @pl.when(at // per == p)
        def _():
            span = pl.ds(pl.multiple_of(at % per * depth, 16), depth)
            pltpu.make_async_copy(part.at[span, :], target, sem).start()


def wait_for(ref, sem):
    pltpu.make_async_copy(ref, ref, sem).wait()


def gate_kernel(parts, first, count, chips, meta, *refs):
    gate_up, pieces = refs[:parts], refs[parts:-5]
    total, held, weight, piece_sems, weight_sems = refs[-5:]
    depth = pieces[0].shape[1]
    for k in range(count):
        side = held.shape[2] // depth
        target = weight.at[k // side, pl.ds(k % side * depth, depth), :]
        weight_start(meta[first + k], gate_up, depth, chips // parts, target, weight_sems.at[k])
        if k == 0:
            piece_starts(pieces, count, held, piece_sems)

    add_products(count, depth, held, weight, total, piece_sems, weight_sems)


def gate(meta, first, pieces, rows, gate_up, chips):
    count = len(pieces[0])
    depth = pieces[0][0].shape[1]
    side = 1 if depth % 128 else 2
    wide = gate_up[0].shape[1]
    return pl.pallas_call(
        functools.partial(gate_kernel, len(gate_up), first, count, chips),
        out_shape=jax.ShapeDtypeStruct((rows, wide), jnp.float32),
        in_specs=[IN_SMEM] + [IN_HBM] * len(gate_up) + [ANY] * (STREAMS * count),
        out_specs=IN_VMEM,
        scratch_shapes=[
            pltpu.VMEM((-(-count // side), rows, side * depth), jnp.bfloat16),
            pltpu.VMEM((-(-count // side), side * depth, wide), jnp.bfloat16),
            pltpu.SemaphoreType.DMA((count,)),
            pltpu.SemaphoreType.DMA((count,)),
        ],
        compiler_params=pltpu.CompilerParams(vmem_limit_bytes=VMEM),
        cost_estimate=pl.CostEstimate(
            flops=2 * rows * count * depth * wide,
            bytes_accessed=2 * count * depth * (wide + rows),
            transcendentals=0,
        ),
    )(meta, *gate_up, *[piece for part in pieces for piece in part])


def tail_kernel(parts, first, count, chips, meta, factors, before, down, *refs):
    gate_up, pieces = refs[:parts], refs[parts : parts + STREAMS * count]
    rest = refs[parts + STREAMS * count :]
    outs = rest[:4]
    held, weight, total, earlier, active, ordered, second, staged = rest[4:12]
    piece_sems, weight_sems, earlier_sem, second_sems, out_sems = rest[12:]
    rows = held.shape[1]
    depth = pieces[0].shape[1]
    hidden = active.shape[1]
    steps, _, span = second.shape
    for k in range(count):
        side = held.shape[2] // depth
        target = weight.at[k // side, pl.ds(k % side * depth, depth), :]
        weight_start(meta[first + k], gate_up, depth, chips // parts, target, weight_sems.at[k])
        if k == 0:
            piece_starts(pieces, count, held, piece_sems)
    pltpu.make_async_copy(before, earlier, earlier_sem).start()

    def columns(n):
        return pl.ds(pl.multiple_of(n * span, span), span)

    @pl.loop(0, steps)
    def _(n):
        pltpu.make_async_copy(down.at[:, columns(n)], second.at[n], second_sems.at[n]).start()

    add_products(count, depth, held, weight, total, piece_sems, weight_sems)

    pltpu.make_async_copy(before, earlier, earlier_sem).wait()
    columns_of = jnp.concatenate([factors[...], jnp.zeros((6, rows), jnp.float32)], axis=0).T
    norm, scale = columns_of[:, 0:1], columns_of[:, 1:2]
    gate = (total[:, :hidden] + earlier[:, :hidden]) * norm
    up = (total[:, hidden:] + earlier[:, hidden:]) * (norm * scale)
    active[...] = (gate * jax.nn.sigmoid(gate) * up).astype(jnp.bfloat16)
    share = rows // (2 * chips)
    for i in range(2 * chips):
        at = pl.ds(pl.multiple_of(meta[chips + 1 + i] * share, share), share)
        ordered[i * share : (i + 1) * share, :] = active[at, :]

    def out_copies(n):
        copies, at = [], 0
        slot = n % 2
        for i, out in enumerate(outs):
            size = out.shape[0]
            source = staged.at[slot, pl.ds(at, size), :]
            copies.append(
                pltpu.make_async_copy(source, out.at[:, columns(n)], out_sems.at[slot, i])
            )
            at += size
        return copies

    @pl.loop(0, steps)
    def _(n):
        pltpu.make_async_copy(down.at[:, columns(n)], second.at[n], second_sems.at[n]).wait()

        @pl.when(n >= 2)
        def _():
            for copy in out_copies(n - 2):
                copy.wait()

        result = jnp.dot(ordered[...], second[n], preferred_element_type=jnp.float32)
        staged[n % 2] = result.astype(jnp.bfloat16)
        for copy in out_copies(n):
            copy.start()

    for n in range(max(0, steps - 2), steps):
        for copy in out_copies(n):
            copy.wait()


def tail(meta, first, pieces, rows, gate_up, before, factors, down, chips):
    count = len(pieces[0])
    depth = pieces[0][0].shape[1]
    side = 1 if depth % 128 else 2
    wide = gate_up[0].shape[1]
    hidden, width = down.shape
    share = rows // (2 * chips)
    steps = max(1, width // 1024)
    shapes = [3 * share, 3 * share, rows // 2 - 3 * share, rows // 2 - 3 * share]
    return pl.pallas_call(
        functools.partial(tail_kernel, len(gate_up), first, count, chips),
        out_shape=tuple(jax.ShapeDtypeStruct((n, width), jnp.bfloat16) for n in shapes),
        in_specs=[IN_SMEM, IN_VMEM, ANY, IN_HBM]
        + [IN_HBM] * len(gate_up)
        + [ANY] * (STREAMS * count),
        out_specs=(ANY,) * 4,
        scratch_shapes=[
            pltpu.VMEM((-(-count // side), rows, side * depth), jnp.bfloat16),
            pltpu.VMEM((-(-count // side), side * depth, wide), jnp.bfloat16),
            pltpu.VMEM((rows, wide), jnp.float32),
            pltpu.VMEM((rows, wide), jnp.float32),
            pltpu.VMEM((rows, hidden), jnp.bfloat16),
            pltpu.VMEM((rows, hidden), jnp.bfloat16),
            pltpu.VMEM((steps, hidden, width // steps), jnp.bfloat16),
            pltpu.VMEM((2, rows, width // steps), jnp.bfloat16),
            pltpu.SemaphoreType.DMA((count,)),
            pltpu.SemaphoreType.DMA((count,)),
            pltpu.SemaphoreType.DMA(()),
            pltpu.SemaphoreType.DMA((steps,)),
            pltpu.SemaphoreType.DMA((2, 4)),
        ],
        compiler_params=pltpu.CompilerParams(vmem_limit_bytes=VMEM),
        cost_estimate=pl.CostEstimate(
            flops=2 * rows * (count * depth * wide + hidden * width),
            bytes_accessed=2 * (count * depth * (wide + rows) + width * (hidden + rows)),
            transcendentals=rows * wide,
        ),
    )(meta, factors, before, down, *gate_up, *[piece for part in pieces for piece in part])


def body(
    hidden_in,
    queries,
    latent_cache,
    new_latent,
    cache_lengths,
    value_up,
    out_proj,
    norm_gain,
    router,
    expert_ids,
    w_gate_up,
    w_down,
):
    rows = hidden_in.shape[0]
    width = hidden_in.shape[1]
    chips = lax.axis_size("chip")
    cores = lax.axis_size("core")
    groups = lax.axis_size(GROUP)
    core = lax.axis_index("core")
    chip = lax.axis_index("chip")
    group = lax.axis_index(GROUP)
    place = chip * cores + core
    chip_cols = width // chips
    own_cols = chip_cols // cores
    expert_count = router.shape[1]
    total = chips * cores * rows
    order = ring_order()

    outgoing = hidden_in.reshape(rows, chips, chip_cols).transpose(1, 0, 2)
    names = jnp.broadcast_to(expert_ids.astype(jnp.bfloat16)[None], (chips, rows, TOP))
    arrived = lax.all_to_all(
        jnp.concatenate([outgoing, names], axis=2), "chip", split_axis=0, concat_axis=0, tiled=True
    )

    parts = 4
    span = width // parts
    gate_up = []
    stages = [None, (0, 0), (1, 0), (0, 1)]
    final = chips // 2 - 1
    ends = [(1, 1), (0, 2), (1, 2), (None, final)]
    projected = []

    def during_first(s, i, moving, pieces):
        if (s, i) == (None, None):
            part = project([piece[: chips - 1] for piece in pieces], out_proj.T, 2, 20 * 1024 * 1024)
            moving, part = lax.optimization_barrier((moving, part))
            projected.append(part)
        if (s, i) in ends:
            p = ends.index((s, i))
            raw = w_gate_up
            if stages[p] is not None:
                raw, _ = lax.optimization_barrier((raw, pieces[stages[p][0]][1 + 2 * stages[p][1]]))
            quarter = raw[0, p * span : (p + 1) * span].reshape(span, -1)
            moving, quarter = lax.optimization_barrier((moving, quarter))
            gate_up.append(quarter)
        return moving

    own_gain = lax.dynamic_slice_in_dim(norm_gain, place * own_cols, own_cols, 0)[None]
    own_router = lax.dynamic_slice_in_dim(router.T, place * own_cols, own_cols, 1)
    first_rows, then_rows = reduce_rows()
    meta = jnp.stack(order + [place] + first_rows + then_rows).astype(jnp.int32)

    head_out = attend(queries, latent_cache, new_latent, cache_lengths, value_up)
    head_out, arrived = lax.optimization_barrier((head_out, arrived))
    other_arrived = swap_cores(arrived)
    low, high = by_core(core, head_out, swap_cores(head_out))
    block = jnp.concatenate([low, high], axis=0)
    half = block.shape[1] // STREAMS
    pieces = ring_gather([block[:, s * half : (s + 1) * half] for s in range(STREAMS)], during_first)
    projected.append(project([piece[chips - 1 :] for piece in pieces], out_proj.T, 8, VMEM))
    parts, got = [], []
    for part in projected:
        if groups == 2:
            parts.append(part)
            got.append(lax.ppermute(part.astype(jnp.bfloat16), "sec", SWAP))
        else:
            parts.append(lax.psum(part, GROUP))
            got.append(jnp.zeros(part.shape, jnp.bfloat16))
    arrived = jnp.stack(by_core(core, arrived, other_arrived), axis=1)
    arrived = arrived.reshape(chips, cores * rows, chip_cols + TOP)
    residual, stats = finish(meta, parts, got, arrived, own_gain, own_router)
    residual = residual.reshape(total, own_cols)
    stats = stats.reshape(total, expert_count + 1).T
    stats = stats + swap_cores(stats)
    low, high = by_core(core, residual, swap_cores(residual))
    block = jnp.concatenate([low, high], axis=1)
    half = total // STREAMS

    ids = arrived[:, :, chip_cols:].reshape(total, TOP).T.astype(jnp.int32)
    grid = lax.broadcasted_iota(jnp.int32, (1, expert_count, 1), 1)
    chosen = jnp.any(ids[:, None, :] == grid, axis=0)

    def packed(sums):
        high = lax.reduce_precision(sums, 8, 7)
        flat = jnp.stack([high, sums - high]).astype(jnp.bfloat16).reshape(-1)
        extra = -(-flat.size // (16 * chip_cols)) * 16
        return jnp.pad(flat, (0, extra * chip_cols - flat.size)).reshape(extra, chip_cols)

    def unpacked(pieces):
        count = expert_count + 1
        added = sum(piece[half:].astype(jnp.float32) for piece in pieces).reshape(-1)
        return jnp.sum(added[: 2 * count * half].reshape(2, count, half), axis=0)

    blocks = []
    for s in range(STREAMS):
        span = slice(s * half, (s + 1) * half)
        blocks.append(jnp.concatenate([block[span], packed(stats[:, span])], axis=0))

    def route(stats):
        norm = lax.rsqrt(stats[expert_count:] / width + norm_epsilon)
        affinity = jnp.where(chosen, jax.nn.sigmoid(stats[:expert_count] * norm), 0.0)
        scale = jnp.sum(jnp.where(grid[0] == place, affinity, 0.0), axis=0, keepdims=True)
        scale = route_scale * scale / jnp.sum(affinity, axis=0, keepdims=True)
        return jnp.concatenate([norm, scale], axis=0)

    sums = []
    def during_second(s, i, moving, pieces):
        if (s, i) == (STREAMS - 1, None):
            moving, sums[0] = lax.optimization_barrier((moving, sums[0]))
        if (s, i) == (STREAMS - 1, final - 1):
            blocks = [piece[: chips - 3] for piece in pieces]
            blocks, _ = lax.optimization_barrier((blocks, moving))
            sums.append(gate(meta, 0, blocks, total, gate_up, chips))
        return moving

    pieces = ring_gather(blocks, during_second)
    stats = jnp.concatenate([unpacked(part) for part in pieces], axis=1)
    keep_first, give_first, keep_then, give_then = tail(
        meta,
        chips - 3,
        [piece[chips - 3 :] for piece in pieces],
        total,
        gate_up,
        sums[0],
        route(stats),
        w_down[0],
        chips,
    )

    got = [swap_cores(give_first), swap_cores(give_then)]

    def own_columns(block):
        held, _ = lax.optimization_barrier((pieces, block))
        own = own_residual(meta, held, rows).reshape(groups, chips // groups, rows, chip_cols)
        own = lax.dynamic_index_in_dim(own, group, 0, keepdims=False)
        own = own.transpose(1, 0, 2).reshape(rows, width // groups).astype(jnp.float32)
        span = width // groups
        return own / lax.dynamic_slice_in_dim(norm_gain, group * span, span, 0)

    mixture, own = ring_reduce([keep_first, keep_then], got, own_columns)
    if groups == 2:
        mixture = plus(*mixture)
    else:
        mixture = jnp.concatenate(mixture, axis=1).reshape(rows, groups, width // groups)
        mixture = lax.psum_scatter(mixture, GROUP, scatter_dimension=1, tiled=False)
    return plus(own, mixture).astype(jnp.bfloat16)


def solution(mesh):
    sec, batch, head = mesh.shape["sec"], mesh.shape["batch"], mesh.shape["head"]
    devices = mesh.devices.reshape(sec, batch // 2, 2, head)
    split = Mesh(devices, ("sec", "chip", "core", "head"))
    tokens = ("chip", "core")
    in_specs = (
        P(tokens, None),
        P(tokens, GROUP, None),
        P(tokens, None, None),
        P(tokens, None),
        P(tokens),
        P(GROUP, None, None),
        P(GROUP, tokens),
        P(),
        P(),
        P(tokens, None),
        P(tokens, None, None, GROUP),
        P(tokens, GROUP, None),
    )
    out_specs = P(tokens, GROUP)
    return jax.shard_map(body, mesh=split, in_specs=in_specs, out_specs=out_specs, check_vma=False)
```

profile of v0, /device:TPU:0, one launch (start us, length us, event | category | flops | bytes accessed | tf_op | source)
XLA Modules:
  0.0 221.5 jit_solution(12717528350835834619)
XLA Ops:
  0.0 1.2 copy.56
  2.9 7.3 %all-to-all-start = ((bf16[8,32,904]{2,1,0:T(8,128)(2,1)}), bf16[8,32,904]{2,1,0:T(8,128)(2,1)S(1)}, u32[]{:S(2)}, u32[]{:S(2)}) async-start(bf16[8,32,904]{2,1,0:T(8,128)(2,1)} %pad_maximum_fusion.2), calls=%async_computation | async-start | bytes 1048576 | tf_op jit(solution)/shard_map/all_to_all | solution.py:572
  11.2 6.7 %fusion.6 = (f32[32,64]{1,0:T(8,128)S(1)}, f32[32,64,192]{2,1,0:T(8,128)S(1)}) fusion(pred[32,192]{1,0:T(8,128)(4,1)S(1)} %iota_compare_fusion.1, bf16[32,64,576]{2,1,0:T(8,128)(2,1)S(1)} %copy-done, bf16[32,192,576]{2,1,0:T(8,128)(2,1)} %param.14), kind=kOutput, calls=%fused_computation.8 | convolution fusion | flops 454162432 | bytes 11024384 | tf_op jit(solution)/shard_map/thk,tjk->thj/dot_general | solution.py:33
  19.0 2.0 add_convert_fusion
  21.7 2.3 %fusion.11 = bf16[64,4,8,128]{3,2,1,0:T(8,128)(2,1)S(1)} fusion(bf16[64,512,128]{2,1,0:T(8,128)(2,1)S(1)} %bitcast.115, bf16[32,64,512]{2,1,0:T(8,128)(2,1)S(1)} %add_convert_fusion), kind=kOutput, calls=%fused_computation.11 | convolution fusion | flops 268697600 | bytes 11010048 | tf_op jit(solution)/shard_map/thc,hcd->thd/dot_general | solution.py:59
  24.7 1.9 collective-permute-done.1
  26.7 1.6 collective-permute-start.5
  28.3 1.5 collective-permute-start.2
  30.4 2.8 %copy.42 = bf16[224,8,2,512]{3,1,2,0:T(8,128)(2,1)} copy(bf16[224,8,2,512]{3,2,1,0:T(2,128)(2,1)S(1)} %bitcast.116) | data formatting | bytes 7340032
  33.2 2.8 %collective-permute-done.5.refs_8_ = bf16[64,4096]{1,0:T(8,128)(2,1)S(1)} collective-permute-done((bf16[64,4096]{1,0:T(8,128)(2,1)S(1)}, bf16[64,4096]{1,0:T(8,128)(2,1)S(1)}, u32[]{:S(2)}, u32[]{:S(2)}) %collective-permute-start.5) | collective-permute-done | bytes 524320 | tf_op jit(solution)/shard_map/ppermute | solution.py:81
  36.0 1.5 collective-permute-start.6
  37.5 4.1 %collective-permute-done.2.refs_1_ = bf16[64,4096]{1,0:T(8,128)(2,1)S(1)} collective-permute-done((bf16[64,4096]{1,0:T(8,128)(2,1)S(1)}, bf16[64,4096]{1,0:T(8,128)(2,1)S(1)}, u32[]{:S(2)}, u32[]{:S(2)}) %collective-permute-start.2) | collective-permute-done | bytes 524320 | tf_op jit(solution)/shard_map/ppermute | solution.py:81
  41.6 1.5 collective-permute-start.3
  43.1 2.8 %copy.43 = bf16[224,8,2,512]{3,1,2,0:T(8,128)(2,1)} copy(bf16[224,8,2,512]{3,2,1,0:T(2,128)(2,1)S(1)} %bitcast.117) | data formatting | bytes 7340032
  45.9 2.0 slice-done.6
  48.0 2.8 %copy.41 = bf16[224,8,2,512]{3,1,2,0:T(8,128)(2,1)} copy(bf16[224,8,2,512]{3,2,1,0:T(2,128)(2,1)S(1)} %bitcast.118) | data formatting | bytes 7340032
  50.8 1.5 collective-permute-start.7
  52.8 1.5 collective-permute-start.4
  54.9 2.9 %copy.44 = bf16[224,8,2,512]{3,1,2,0:T(8,128)(2,1)} copy(bf16[224,8,2,512]{3,2,1,0:T(2,128)(2,1)S(1)} %bitcast.119) | data formatting | bytes 7340032
  58.3 1.7 collective-permute-done.7.refs_12_
  60.0 5.6 %collective-permute-done.4.refs_5_ = bf16[64,4096]{1,0:T(8,128)(2,1)S(1)} collective-permute-done((bf16[64,4096]{1,0:T(8,128)(2,1)S(1)}, bf16[64,4096]{1,0:T(8,128)(2,1)S(1)}, u32[]{:S(2)}, u32[]{:S(2)}) %collective-permute-start.4) | collective-permute-done | bytes 524320 | tf_op jit(solution)/shard_map/ppermute | solution.py:81
  65.7 1.7 collective-permute-start.8
  67.5 6.9 %shard_map.118.refs_0_ = f32[448,448]{1,0:T(8,128)S(1)} custom-call(bf16[448,8192]{1,0:T(8,128)(2,1)S(1)} %bitcast.100, bf16[64,4096]{1,0:T(8,128)(2,1)S(1)} %get-tuple-element.134.refs_0_, bf16[64,4096]{1,0:T(8,128)(2,1)S(1)} %collective-permute-done.2.refs_1_, bf16[64,4096]{1,0:T(8,128)(2,1)S(1)} %collective-permute-done.9.refs_2_, ...), custom_call_target="tpu_custom_call" | custom-call | flops 3288334336 | bytes 15482880 | tf_op jit(solution)/shard_map/pallas_call | solution.py:247
  76.2 1.1 select_bitcast_fusion.1
  77.4 1.6 collective-permute-start.16
  79.0 2.1 broadcast_select_fusion.4
  81.1 7.1 %shard_map.119.refs_1_ = f32[64,448]{1,0:T(8,128)} custom-call(bf16[448,8192]{1,0:T(8,128)(2,1)} %bitcast.97, bf16[64,4096]{1,0:T(8,128)(2,1)} %get-tuple-element.132.refs_0_, bf16[64,4096]{1,0:T(8,128)(2,1)} %get-tuple-element.131.refs_1_), custom_call_target="tpu_custom_call" | custom-call | flops 469762048 | bytes 8503296 | tf_op jit(solution)/shard_map/pallas_call | solution.py:247
  90.4 3.1 %collective-permute-done.17.refs_3_ = bf16[64,448]{1,0:T(8,128)(2,1)S(1)} collective-permute-done((bf16[64,448]{1,0:T(8,128)(2,1)S(1)}, bf16[64,448]{1,0:T(8,128)(2,1)S(1)}, u32[]{:S(2)}, u32[]{:S(2)}) %collective-permute-start.17) | collective-permute-done | bytes 57376 | tf_op jit(solution)/shard_map/ppermute | solution.py:616
  93.6 1.3 shard_map.120
  97.5 1.5 collective-permute-start.25
  99.1 1.5 collective-permute-start.20
  100.6 5.8 %collective-permute-done.25.refs_10_.refs_9_ = bf16[272,896]{1,0:T(8,128)(2,1)S(1)} collective-permute-done((bf16[272,896]{1,0:T(8,128)(2,1)S(1)}, bf16[272,896]{1,0:T(8,128)(2,1)S(1)}, u32[]{:S(2)}, u32[]{:S(2)}) %collective-permute-start.25) | collective-permute-done | bytes 487456 | tf_op jit(solution)/shard_map/ppermute | solution.py:81
  106.3 1.5 collective-permute-start.26
  107.8 3.8 %collective-permute-done.20.refs_5_.refs_1_ = bf16[272,896]{1,0:T(8,128)(2,1)S(1)} collective-permute-done((bf16[272,896]{1,0:T(8,128)(2,1)S(1)}, bf16[272,896]{1,0:T(8,128)(2,1)S(1)}, u32[]{:S(2)}, u32[]{:S(2)}) %collective-permute-start.20) | collective-permute-done | bytes 487456 | tf_op jit(solution)/shard_map/ppermute | solution.py:81
  111.5 1.5 collective-permute-start.22
  113.5 3.2 %collective-permute-done.26.refs_12_.refs_11_ = bf16[272,896]{1,0:T(8,128)(2,1)S(1)} collective-permute-done((bf16[272,896]{1,0:T(8,128)(2,1)S(1)}, bf16[272,896]{1,0:T(8,128)(2,1)S(1)}, u32[]{:S(2)}, u32[]{:S(2)}) %collective-permute-start.26) | collective-permute-done | bytes 487456 | tf_op jit(solution)/shard_map/ppermute | solution.py:81
  116.8 5.2 %collective-permute-done.22.refs_7_.refs_3_ = bf16[272,896]{1,0:T(8,128)(2,1)S(1)} collective-permute-done((bf16[272,896]{1,0:T(8,128)(2,1)S(1)}, bf16[272,896]{1,0:T(8,128)(2,1)S(1)}, u32[]{:S(2)}, u32[]{:S(2)}) %collective-permute-start.22) | collective-permute-done | bytes 487456 | tf_op jit(solution)/shard_map/ppermute | solution.py:81
  122.0 1.5 collective-permute-start.27
  123.5 1.4 collective-permute-start.24
  126.7 10.5 %shard_map.121.before = f32[512,1024]{1,0:T(8,128)} custom-call(s32[25]{0:T(128)} %copy-done.3, bf16[1792,1024]{1,0:T(8,128)(2,1)} %bitcast.106, bf16[1792,1024]{1,0:T(8,128)(2,1)} %bitcast.110, bf16[1792,1024]{1,0:T(8,128)(2,1)} %bitcast.108, bf16[1792,1024]{1,0:T(8,128)(2,1)} %bitcast.112, bf16[272,896]{1,0:T(8,128)(2,1)} %copy-done.9, ...), custom_call_target="tpu_custom_call" | custom-call | flops 4697620480 | bytes 13762560 | tf_op jit(solution)/shard_map/pallas_call | solution.py:412
  137.4 2.2 collective-permute-start.31
  139.6 6.6 %collective-permute-done.31 = bf16[272,896]{1,0:T(8,128)(2,1)S(1)} collective-permute-done((bf16[272,896]{1,0:T(8,128)(2,1)S(1)}, bf16[272,896]{1,0:T(8,128)(2,1)S(1)}, u32[]{:S(2)}, u32[]{:S(2)}) %collective-permute-start.31) | collective-permute-done | bytes 487456 | tf_op jit(solution)/shard_map/ppermute | solution.py:81
  148.2 1.3 broadcast_select_fusion.8
  152.4 14.2 %shard_map.122 = (bf16[96,7168]{1,0:T(8,128)(2,1)}, bf16[96,7168]{1,0:T(8,128)(2,1)}, bf16[160,7168]{1,0:T(8,128)(2,1)}, bf16[160,7168]{1,0:T(8,128)(2,1)}) custom-call(s32[25]{0:T(128)} %copy-done.3, f32[2,512]{1,0:T(2,128)} %pad_maximum_fusion.9.factors, f32[512,1024]{1,0:T(8,128)} %shard_map.121.before, bf16[512,7168]{1,0:T(8,128)(2,1)} %bitcast.122, ...), custom_call_target="tpu_custom_call" | custom-call | flops 6576668672 | bytes 22937600 | tf_op jit(solution)/shard_map/pallas_call | solution.py:510
  166.8 3.3 %collective-permute-done.35 = bf16[96,7168]{1,0:T(8,128)(2,1)} collective-permute-done((bf16[96,7168]{1,0:T(8,128)(2,1)}, bf16[96,7168]{1,0:T(8,128)(2,1)}, u32[]{:S(2)}, u32[]{:S(2)}) %collective-permute-start.35) | collective-permute-done | bytes 1376288 | tf_op jit(solution)/shard_map/ppermute | solution.py:85
  170.2 1.4 add_convert_fusion.9
  171.6 2.2 %collective-permute-start.36 = (bf16[32,3584]{1,0:T(8,128)(2,1)S(1)}, bf16[32,3584]{1,0:T(8,128)(2,1)S(1)}, u32[]{:S(2)}, u32[]{:S(2)}) collective-permute-start(bf16[32,3584]{1,0:T(8,128)(2,1)S(1)} %get-tuple-element.128), channel_id=1, source_target_pairs={{0,4},{5,1},{4,8},{9,5},{8,12},{13,9},{12,14},{15,13},{14,10},{11,... | collective-permute-start | bytes 688136 | tf_op jit(solution)/shard_map/ppermute | solution.py:81
  174.3 3.4 %collective-permute-done.36 = bf16[32,3584]{1,0:T(8,128)(2,1)S(1)} collective-permute-done((bf16[32,3584]{1,0:T(8,128)(2,1)S(1)}, bf16[32,3584]{1,0:T(8,128)(2,1)S(1)}, u32[]{:S(2)}, u32[]{:S(2)}) %collective-permute-start.36) | collective-permute-done | bytes 229408 | tf_op jit(solution)/shard_map/ppermute | solution.py:81
  177.6 2.5 %collective-permute-done.37 = bf16[32,3584]{1,0:T(8,128)(2,1)S(1)} collective-permute-done((bf16[32,3584]{1,0:T(8,128)(2,1)S(1)}, bf16[32,3584]{1,0:T(8,128)(2,1)S(1)}, u32[]{:S(2)}, u32[]{:S(2)}) %collective-permute-start.37) | collective-permute-done | bytes 229408 | tf_op jit(solution)/shard_map/ppermute | solution.py:81
  180.2 1.2 add_convert_fusion.6
  181.4 2.2 %collective-permute-start.39 = (bf16[64,3584]{1,0:T(8,128)(2,1)S(1)}, bf16[64,3584]{1,0:T(8,128)(2,1)S(1)}, u32[]{:S(2)}, u32[]{:S(2)}) collective-permute-start(bf16[64,3584]{1,0:T(8,128)(2,1)S(1)} %add_convert_fusion.6), channel_id=1, source_target_pairs={{0,4},{5,1},{4,8},{9,5},{8,12},{13,9},{12,14},{15,13},{14,10},{11,... | collective-permute-start | bytes 1376264 | tf_op jit(solution)/shard_map/ppermute | solution.py:81
  183.7 1.2 add_convert_fusion.5
  185.3 2.5 %shard_map.123 = bf16[8,32,896]{2,1,0:T(8,128)(2,1)} custom-call(s32[25]{0:T(128)} %copy-done.3, bf16[272,896]{1,0:T(8,128)(2,1)} %copy-done.9, bf16[272,896]{1,0:T(8,128)(2,1)} %copy-done.12, bf16[272,896]{1,0:T(8,128)(2,1)} %copy-done.16, bf16[272,896]{1,0:T(8,128)(2,1)} %copy-done.14, bf16[272,896]{1,0:T(8,128)(2,1)} %copy-done.18, ...), custom_call_target="tpu_custom_call" | custom-call | tf_op jit(solution)/shard_map/pallas_call | solution.py:328
  187.9 1.1 convert_bitcast_fusion
  190.1 2.2 %collective-permute-start.41 = (bf16[64,3584]{1,0:T(8,128)(2,1)S(1)}, bf16[64,3584]{1,0:T(8,128)(2,1)S(1)}, u32[]{:S(2)}, u32[]{:S(2)}) collective-permute-start(bf16[64,3584]{1,0:T(8,128)(2,1)S(1)} %add_convert_fusion.4), channel_id=1, source_target_pairs={{0,4},{5,1},{4,8},{9,5},{8,12},{13,9},{12,14},{15,13},{14,10},{11,... | collective-permute-start | bytes 1376264 | tf_op jit(solution)/shard_map/ppermute | solution.py:81
  192.4 2.5 %collective-permute-done.38 = bf16[64,3584]{1,0:T(8,128)(2,1)S(1)} collective-permute-done((bf16[64,3584]{1,0:T(8,128)(2,1)S(1)}, bf16[64,3584]{1,0:T(8,128)(2,1)S(1)}, u32[]{:S(2)}, u32[]{:S(2)}) %collective-permute-start.38) | collective-permute-done | bytes 458784 | tf_op jit(solution)/shard_map/ppermute | solution.py:81
  195.0 2.2 %collective-permute-start.40 = (bf16[64,3584]{1,0:T(8,128)(2,1)S(1)}, bf16[64,3584]{1,0:T(8,128)(2,1)S(1)}, u32[]{:S(2)}, u32[]{:S(2)}) collective-permute-start(bf16[64,3584]{1,0:T(8,128)(2,1)S(1)} %add_convert_fusion.3), channel_id=1, source_target_pairs={{0,4},{5,1},{4,8},{9,5},{8,12},{13,9},{12,14},{15,13},{14,10},{11,... | collective-permute-start | bytes 1376264 | tf_op jit(solution)/shard_map/ppermute | solution.py:81
  197.2 2.5 %collective-permute-done.41 = bf16[64,3584]{1,0:T(8,128)(2,1)S(1)} collective-permute-done((bf16[64,3584]{1,0:T(8,128)(2,1)S(1)}, bf16[64,3584]{1,0:T(8,128)(2,1)S(1)}, u32[]{:S(2)}, u32[]{:S(2)}) %collective-permute-start.41) | collective-permute-done | bytes 458784 | tf_op jit(solution)/shard_map/ppermute | solution.py:81
  200.0 2.2 %collective-permute-start.42 = (bf16[64,3584]{1,0:T(8,128)(2,1)S(1)}, bf16[64,3584]{1,0:T(8,128)(2,1)S(1)}, u32[]{:S(2)}, u32[]{:S(2)}) collective-permute-start(bf16[64,3584]{1,0:T(8,128)(2,1)S(1)} %add_convert_fusion.2), channel_id=1, source_target_pairs={{0,4},{5,1},{4,8},{9,5},{8,12},{13,9},{12,14},{15,13},{14,10},{11,... | collective-permute-start | bytes 1376264 | tf_op jit(solution)/shard_map/ppermute | solution.py:81
  202.2 2.5 %collective-permute-done.40 = bf16[64,3584]{1,0:T(8,128)(2,1)S(1)} collective-permute-done((bf16[64,3584]{1,0:T(8,128)(2,1)S(1)}, bf16[64,3584]{1,0:T(8,128)(2,1)S(1)}, u32[]{:S(2)}, u32[]{:S(2)}) %collective-permute-start.40) | collective-permute-done | bytes 458784 | tf_op jit(solution)/shard_map/ppermute | solution.py:81
  204.7 4.9 %collective-permute-done.42 = bf16[64,3584]{1,0:T(8,128)(2,1)S(1)} collective-permute-done((bf16[64,3584]{1,0:T(8,128)(2,1)S(1)}, bf16[64,3584]{1,0:T(8,128)(2,1)S(1)}, u32[]{:S(2)}, u32[]{:S(2)}) %collective-permute-start.42) | collective-permute-done | bytes 458784 | tf_op jit(solution)/shard_map/ppermute | solution.py:81
  209.9 2.2 %collective-permute-start.45 = (bf16[64,3584]{1,0:T(8,128)(2,1)S(1)}, bf16[64,3584]{1,0:T(8,128)(2,1)S(1)}, u32[]{:S(2)}, u32[]{:S(2)}) collective-permute-start(bf16[64,3584]{1,0:T(8,128)(2,1)S(1)} %add_convert_fusion.1), channel_id=1, source_target_pairs={{0,4},{5,1},{4,8},{9,5},{8,12},{13,9},{12,14},{15,13},{14,10},{11,... | collective-permute-start | bytes 1376264 | tf_op jit(solution)/shard_map/ppermute | solution.py:81
  212.9 5.6 %collective-permute-done.45 = bf16[64,3584]{1,0:T(8,128)(2,1)S(1)} collective-permute-done((bf16[64,3584]{1,0:T(8,128)(2,1)S(1)}, bf16[64,3584]{1,0:T(8,128)(2,1)S(1)}, u32[]{:S(2)}, u32[]{:S(2)}) %collective-permute-start.45) | collective-permute-done | bytes 458784 | tf_op jit(solution)/shard_map/ppermute | solution.py:81
  219.2 1.5 collective-permute-done.46
  (196 shorter events, 26.5 us)
Async XLA Ops:
  0.0 10.3 %copy-start = (bf16[32,64,576]{2,1,0:T(8,128)(2,1)S(1)}, bf16[32,64,576]{2,1,0:T(8,128)(2,1)}, u32[]{:S(2)}) copy-start(bf16[32,64,576]{2,1,0:T(8,128)(2,1)} %param.13) | copy-start | bytes 7077892
  0.0 10.2 %copy-start.25 = (s32[32]{0:T(128)S(1)}, s32[32]{0:T(128)}, u32[]{:S(2)}) copy-start(s32[32]{0:T(128)} %param.16) | copy-start | bytes 388
  0.0 10.2 %copy-start.23 = (bf16[32,576]{1,0:T(8,128)(2,1)S(1)}, bf16[32,576]{1,0:T(8,128)(2,1)}, u32[]{:S(2)}) copy-start(bf16[32,576]{1,0:T(8,128)(2,1)} %param.15) | copy-start | bytes 110596
  2.9 21.8 %all-to-all-start = ((bf16[8,32,904]{2,1,0:T(8,128)(2,1)}), bf16[8,32,904]{2,1,0:T(8,128)(2,1)S(1)}, u32[]{:S(2)}, u32[]{:S(2)}) async-start(bf16[8,32,904]{2,1,0:T(8,128)(2,1)} %pad_maximum_fusion.2), calls=%async_computation | async-start | bytes 1048576 | tf_op jit(solution)/shard_map/all_to_all | solution.py:572
  10.3 8.7 %slice-start.8 = ((s8[7864320]{0:T(1024)(128)(4,1)}), s8[4194304]{0:T(1024)(128)(4,1)S(1)}, s32[]{:S(2)}) async-start(s8[7864320]{0:T(1024)(128)(4,1)} %bitcast.120), calls=%async_computation.9 | async-start | bytes 8388608
  24.7 1.9 collective-permute-start.1
  26.7 9.2 %collective-permute-start.5 = (bf16[64,4096]{1,0:T(8,128)(2,1)S(1)}, bf16[64,4096]{1,0:T(8,128)(2,1)S(1)}, u32[]{:S(2)}, u32[]{:S(2)}) collective-permute-start(bf16[64,4096]{1,0:T(8,128)(2,1)S(1)} %get-tuple-element.133.refs_7_), channel_id=1, source_target_pairs={{0,4},{5,1},{4,8},{9,5},{8,12},{13,9},{12,14},{15,13},{14,10},{11,... | collective-permute-start | bytes 1572872 | tf_op jit(solution)/shard_map/ppermute | solution.py:81
  28.3 13.3 %collective-permute-start.2 = (bf16[64,4096]{1,0:T(8,128)(2,1)S(1)}, bf16[64,4096]{1,0:T(8,128)(2,1)S(1)}, u32[]{:S(2)}, u32[]{:S(2)}) collective-permute-start(bf16[64,4096]{1,0:T(8,128)(2,1)S(1)} %get-tuple-element.134.refs_0_), channel_id=1, source_target_pairs={{0,4},{5,1},{4,8},{9,5},{8,12},{13,9},{12,14},{15,13},{14,10},{11,... | collective-permute-start | bytes 1572872 | tf_op jit(solution)/shard_map/ppermute | solution.py:81
  36.0 14.8 %collective-permute-start.6 = (bf16[64,4096]{1,0:T(8,128)(2,1)S(1)}, bf16[64,4096]{1,0:T(8,128)(2,1)S(1)}, u32[]{:S(2)}, u32[]{:S(2)}) collective-permute-start(bf16[64,4096]{1,0:T(8,128)(2,1)S(1)} %collective-permute-done.5.refs_8_), channel_id=1, source_target_pairs={{0,4},{5,1},{4,8},{9,5},{8,12},{13,9},{12,14},{15,13},{14,10},{11,... | collective-permute-start | bytes 1572872 | tf_op jit(solution)/shard_map/ppermute | solution.py:81
  41.6 11.2 %collective-permute-start.3 = (bf16[64,4096]{1,0:T(8,128)(2,1)S(1)}, bf16[64,4096]{1,0:T(8,128)(2,1)S(1)}, u32[]{:S(2)}, u32[]{:S(2)}) collective-permute-start(bf16[64,4096]{1,0:T(8,128)(2,1)S(1)} %collective-permute-done.2.refs_1_), channel_id=1, source_target_pairs={{0,4},{5,1},{4,8},{9,5},{8,12},{13,9},{12,14},{15,13},{14,10},{11,... | collective-permute-start | bytes 1572872 | tf_op jit(solution)/shard_map/ppermute | solution.py:81
  50.8 7.0 %collective-permute-start.12 = (bf16[64,4096]{1,0:T(8,128)(2,1)S(1)}, bf16[64,4096]{1,0:T(8,128)(2,1)S(1)}, u32[]{:S(2)}, u32[]{:S(2)}) collective-permute-start(bf16[64,4096]{1,0:T(8,128)(2,1)S(1)} %collective-permute-done.5.refs_8_), channel_id=1, source_target_pairs={{0,1},{1,0},{2,3},{3,2},{4,5},{5,4},{6,7},{7,6},{8,9},{9,8},{10,11... | collective-permute-start | bytes 1572872 | tf_op jit(solution)/shard_map/ppermute | solution.py:85
  50.8 9.2 %collective-permute-start.7 = (bf16[64,4096]{1,0:T(8,128)(2,1)S(1)}, bf16[64,4096]{1,0:T(8,128)(2,1)S(1)}, u32[]{:S(2)}, u32[]{:S(2)}) collective-permute-start(bf16[64,4096]{1,0:T(8,128)(2,1)S(1)} %collective-permute-done.6.refs_10_), channel_id=1, source_target_pairs={{0,4},{5,1},{4,8},{9,5},{8,12},{13,9},{12,14},{15,13},{14,10},{11,... | collective-permute-start | bytes 1572872 | tf_op jit(solution)/shard_map/ppermute | solution.py:81
  52.8 12.8 %collective-permute-start.4 = (bf16[64,4096]{1,0:T(8,128)(2,1)S(1)}, bf16[64,4096]{1,0:T(8,128)(2,1)S(1)}, u32[]{:S(2)}, u32[]{:S(2)}) collective-permute-start(bf16[64,4096]{1,0:T(8,128)(2,1)S(1)} %collective-permute-done.3.refs_3_), channel_id=1, source_target_pairs={{0,4},{5,1},{4,8},{9,5},{8,12},{13,9},{12,14},{15,13},{14,10},{11,... | collective-permute-start | bytes 1572872 | tf_op jit(solution)/shard_map/ppermute | solution.py:81
  54.4 11.3 %collective-permute-start.9 = (bf16[64,4096]{1,0:T(8,128)(2,1)S(1)}, bf16[64,4096]{1,0:T(8,128)(2,1)S(1)}, u32[]{:S(2)}, u32[]{:S(2)}) collective-permute-start(bf16[64,4096]{1,0:T(8,128)(2,1)S(1)} %collective-permute-done.2.refs_1_), channel_id=1, source_target_pairs={{0,1},{1,0},{2,3},{3,2},{4,5},{5,4},{6,7},{7,6},{8,9},{9,8},{10,11... | collective-permute-start | bytes 1572872 | tf_op jit(solution)/shard_map/ppermute | solution.py:85
  54.4 13.2 %slice-start = ((s8[7340032]{0:T(1024)(128)(4,1)}), s8[4194304]{0:T(1024)(128)(4,1)S(1)}, s32[]{:S(2)}) async-start(s8[7340032]{0:T(1024)(128)(4,1)} %bitcast.98), calls=%async_computation.1 | async-start | bytes 8388608
  54.9 12.7 %slice-start.1 = ((s8[7340032]{0:T(1024)(128)(4,1)}), s8[3145728]{0:T(1024)(128)(4,1)S(1)}, s32[]{:S(2)}) async-start(s8[7340032]{0:T(1024)(128)(4,1)} %bitcast.98), calls=%async_computation.2 | async-start | bytes 6291456
  57.8 9.6 %collective-permute-start.13 = (bf16[64,4096]{1,0:T(8,128)(2,1)S(1)}, bf16[64,4096]{1,0:T(8,128)(2,1)S(1)}, u32[]{:S(2)}, u32[]{:S(2)}) collective-permute-start(bf16[64,4096]{1,0:T(8,128)(2,1)S(1)} %collective-permute-done.6.refs_10_), channel_id=1, source_target_pairs={{0,1},{1,0},{2,3},{3,2},{4,5},{5,4},{6,7},{7,6},{8,9},{9,8},{10,11... | collective-permute-start | bytes 1572872 | tf_op jit(solution)/shard_map/ppermute | solution.py:85
  57.8 9.6 %collective-permute-start.10 = (bf16[64,4096]{1,0:T(8,128)(2,1)S(1)}, bf16[64,4096]{1,0:T(8,128)(2,1)S(1)}, u32[]{:S(2)}, u32[]{:S(2)}) collective-permute-start(bf16[64,4096]{1,0:T(8,128)(2,1)S(1)} %collective-permute-done.3.refs_3_), channel_id=1, source_target_pairs={{0,1},{1,0},{2,3},{3,2},{4,5},{5,4},{6,7},{7,6},{8,9},{9,8},{10,11... | collective-permute-start | bytes 1572872 | tf_op jit(solution)/shard_map/ppermute | solution.py:85
  60.0 7.4 %collective-permute-start.14 = (bf16[64,4096]{1,0:T(8,128)(2,1)S(1)}, bf16[64,4096]{1,0:T(8,128)(2,1)S(1)}, u32[]{:S(2)}, u32[]{:S(2)}) collective-permute-start(bf16[64,4096]{1,0:T(8,128)(2,1)S(1)} %collective-permute-done.7.refs_12_), channel_id=1, source_target_pairs={{0,1},{1,0},{2,3},{3,2},{4,5},{5,4},{6,7},{7,6},{8,9},{9,8},{10,11... | collective-permute-start | bytes 1572872 | tf_op jit(solution)/shard_map/ppermute | solution.py:85
  65.6 1.9 collective-permute-start.11
  65.7 9.5 %collective-permute-start.8 = (bf16[64,4096]{1,0:T(8,128)(2,1)S(1)}, bf16[64,4096]{1,0:T(8,128)(2,1)}, u32[]{:S(2)}, u32[]{:S(2)}) collective-permute-start(bf16[64,4096]{1,0:T(8,128)(2,1)S(1)} %broadcast_select_fusion.6), channel_id=1, source_target_pairs={{0,4},{5,1},{4,8},{9,5},{8,12},{13,9},{12,14},{15,13},{14,10},{11,... | collective-permute-start | bytes 1572872 | tf_op jit(solution)/shard_map/ppermute | solution.py:81
  67.4 8.8 %collective-permute-start = (bf16[8,32,904]{2,1,0:T(8,128)(2,1)S(1)}, bf16[8,32,904]{2,1,0:T(8,128)(2,1)}, u32[]{:S(2)}, u32[]{:S(2)}) collective-permute-start(bf16[8,32,904]{2,1,0:T(8,128)(2,1)S(1)} %all-to-all-done), channel_id=1, source_target_pairs={{0,1},{1,0},{2,3},{3,2},{4,5},{5,4},{6,7},{7,6},{8,9},{9,8},{10,11... | collective-permute-start | bytes 1388552 | tf_op jit(solution)/shard_map/ppermute | solution.py:85
  75.2 3.8 %collective-permute-start.15 = (bf16[64,4096]{1,0:T(8,128)(2,1)}, bf16[64,4096]{1,0:T(8,128)(2,1)S(1)}, u32[]{:S(2)}, u32[]{:S(2)}) collective-permute-start(bf16[64,4096]{1,0:T(8,128)(2,1)} %collective-permute-done.8), channel_id=1, source_target_pairs={{0,1},{1,0},{2,3},{3,2},{4,5},{5,4},{6,7},{7,6},{8,9},{9,8},{10,11... | collective-permute-start | bytes 1572872 | tf_op jit(solution)/shard_map/ppermute | solution.py:85
  75.4 18.1 %copy-start.3 = (s32[25]{0:T(128)}, s32[25]{0:T(128)S(1)}, u32[]{:S(2)}) copy-start(s32[25]{0:T(128)S(1)} %stack.133.meta) | copy-start | bytes 304
  77.4 13.0 %collective-permute-start.16 = (bf16[448,448]{1,0:T(8,128)(2,1)S(1)}, bf16[448,448]{1,0:T(8,128)(2,1)S(1)}, u32[]{:S(2)}, u32[]{:S(2)}) collective-permute-start(bf16[448,448]{1,0:T(8,128)(2,1)S(1)} %convert_element_type.250), channel_id=1, source_target_pairs={{0,16},{16,0},{1,17},{17,1},{2,18},{18,2},{3,19},{19,3},{4,20},{20... | collective-permute-start | bytes 1204232 | tf_op jit(solution)/shard_map/ppermute | solution.py:616
  89.2 4.3 %collective-permute-start.17 = (bf16[64,448]{1,0:T(8,128)(2,1)S(1)}, bf16[64,448]{1,0:T(8,128)(2,1)S(1)}, u32[]{:S(2)}, u32[]{:S(2)}) collective-permute-start(bf16[64,448]{1,0:T(8,128)(2,1)S(1)} %convert_element_type.251), channel_id=1, source_target_pairs={{0,16},{16,0},{1,17},{17,1},{2,18},{18,2},{3,19},{19,3},{4,20},{20... | collective-permute-start | bytes 172040 | tf_op jit(solution)/shard_map/ppermute | solution.py:616
  95.0 1.3 collective-permute-start.18
  95.0 2.0 collective-permute-start.19
  97.5 27.5 %copy-start.8 = (bf16[272,896]{1,0:T(8,128)(2,1)}, bf16[272,896]{1,0:T(8,128)(2,1)S(1)}, u32[]{:S(2)}) copy-start(bf16[272,896]{1,0:T(8,128)(2,1)S(1)} %fusion.20.refs_9_.refs_8_) | copy-start | bytes 1462276
  97.5 8.8 %collective-permute-start.25 = (bf16[272,896]{1,0:T(8,128)(2,1)S(1)}, bf16[272,896]{1,0:T(8,128)(2,1)S(1)}, u32[]{:S(2)}, u32[]{:S(2)}) collective-permute-start(bf16[272,896]{1,0:T(8,128)(2,1)S(1)} %fusion.20.refs_9_.refs_8_), channel_id=1, source_target_pairs={{0,4},{5,1},{4,8},{9,5},{8,12},{13,9},{12,14},{15,13},{14,10},{11,... | collective-permute-start | bytes 1462280 | tf_op jit(solution)/shard_map/ppermute | solution.py:81
  99.0 25.9 %copy-start.9 = (bf16[272,896]{1,0:T(8,128)(2,1)}, bf16[272,896]{1,0:T(8,128)(2,1)S(1)}, u32[]{:S(2)}) copy-start(bf16[272,896]{1,0:T(8,128)(2,1)S(1)} %pad_maximum_fusion.4.refs_4_.refs_0_) | copy-start | bytes 1462276
  99.1 12.5 %collective-permute-start.20 = (bf16[272,896]{1,0:T(8,128)(2,1)S(1)}, bf16[272,896]{1,0:T(8,128)(2,1)S(1)}, u32[]{:S(2)}, u32[]{:S(2)}) collective-permute-start(bf16[272,896]{1,0:T(8,128)(2,1)S(1)} %pad_maximum_fusion.4.refs_4_.refs_0_), channel_id=1, source_target_pairs={{0,4},{5,1},{4,8},{9,5},{8,12},{13,9},{12,14},{15,13},{14,10},{11,... | collective-permute-start | bytes 1462280 | tf_op jit(solution)/shard_map/ppermute | solution.py:81
  106.3 18.6 %copy-start.11 = (bf16[272,896]{1,0:T(8,128)(2,1)}, bf16[272,896]{1,0:T(8,128)(2,1)S(1)}, u32[]{:S(2)}) copy-start(bf16[272,896]{1,0:T(8,128)(2,1)S(1)} %collective-permute-done.25.refs_10_.refs_9_) | copy-start | bytes 1462276
  106.3 10.4 %collective-permute-start.26 = (bf16[272,896]{1,0:T(8,128)(2,1)S(1)}, bf16[272,896]{1,0:T(8,128)(2,1)S(1)}, u32[]{:S(2)}, u32[]{:S(2)}) collective-permute-start(bf16[272,896]{1,0:T(8,128)(2,1)S(1)} %collective-permute-done.25.refs_10_.refs_9_), channel_id=1, source_target_pairs={{0,4},{5,1},{4,8},{9,5},{8,12},{13,9},{12,14},{15,13},{14,10},{11,... | collective-permute-start | bytes 1462280 | tf_op jit(solution)/shard_map/ppermute | solution.py:81
  111.5 13.4 %copy-start.12 = (bf16[272,896]{1,0:T(8,128)(2,1)}, bf16[272,896]{1,0:T(8,128)(2,1)S(1)}, u32[]{:S(2)}) copy-start(bf16[272,896]{1,0:T(8,128)(2,1)S(1)} %collective-permute-done.20.refs_5_.refs_1_) | copy-start | bytes 1462276
  111.5 10.4 %collective-permute-start.22 = (bf16[272,896]{1,0:T(8,128)(2,1)S(1)}, bf16[272,896]{1,0:T(8,128)(2,1)S(1)}, u32[]{:S(2)}, u32[]{:S(2)}) collective-permute-start(bf16[272,896]{1,0:T(8,128)(2,1)S(1)} %collective-permute-done.20.refs_5_.refs_1_), channel_id=1, source_target_pairs={{0,4},{5,1},{4,8},{9,5},{8,12},{13,9},{12,14},{15,13},{14,10},{11,... | collective-permute-start | bytes 1462280 | tf_op jit(solution)/shard_map/ppermute | solution.py:81
  113.0 10.5 %collective-permute-start.28 = (bf16[272,896]{1,0:T(8,128)(2,1)S(1)}, bf16[272,896]{1,0:T(8,128)(2,1)S(1)}, u32[]{:S(2)}, u32[]{:S(2)}) collective-permute-start(bf16[272,896]{1,0:T(8,128)(2,1)S(1)} %collective-permute-done.25.refs_10_.refs_9_), channel_id=1, source_target_pairs={{0,1},{1,0},{2,3},{3,2},{4,5},{5,4},{6,7},{7,6},{8,9},{9,8},{10,11... | collective-permute-start | bytes 1462280 | tf_op jit(solution)/shard_map/ppermute | solution.py:85
  113.0 11.9 %collective-permute-start.21 = (bf16[272,896]{1,0:T(8,128)(2,1)S(1)}, bf16[272,896]{1,0:T(8,128)(2,1)S(1)}, u32[]{:S(2)}, u32[]{:S(2)}) collective-permute-start(bf16[272,896]{1,0:T(8,128)(2,1)S(1)} %collective-permute-done.20.refs_5_.refs_1_), channel_id=1, source_target_pairs={{0,1},{1,0},{2,3},{3,2},{4,5},{5,4},{6,7},{7,6},{8,9},{9,8},{10,11... | collective-permute-start | bytes 1462280 | tf_op jit(solution)/shard_map/ppermute | solution.py:85
  116.8 8.2 %copy-start.13 = (bf16[272,896]{1,0:T(8,128)(2,1)}, bf16[272,896]{1,0:T(8,128)(2,1)S(1)}, u32[]{:S(2)}) copy-start(bf16[272,896]{1,0:T(8,128)(2,1)S(1)} %collective-permute-done.26.refs_12_.refs_11_) | copy-start | bytes 1462276
  116.8 8.2 %collective-permute-start.29 = (bf16[272,896]{1,0:T(8,128)(2,1)S(1)}, bf16[272,896]{1,0:T(8,128)(2,1)S(1)}, u32[]{:S(2)}, u32[]{:S(2)}) collective-permute-start(bf16[272,896]{1,0:T(8,128)(2,1)S(1)} %collective-permute-done.26.refs_12_.refs_11_), channel_id=1, source_target_pairs={{0,1},{1,0},{2,3},{3,2},{4,5},{5,4},{6,7},{7,6},{8,9},{9,8},{10,11... | collective-permute-start | bytes 1462280 | tf_op jit(solution)/shard_map/ppermute | solution.py:85
  122.0 2.9 %collective-permute-start.23 = (bf16[272,896]{1,0:T(8,128)(2,1)S(1)}, bf16[272,896]{1,0:T(8,128)(2,1)S(1)}, u32[]{:S(2)}, u32[]{:S(2)}) collective-permute-start(bf16[272,896]{1,0:T(8,128)(2,1)S(1)} %collective-permute-done.22.refs_7_.refs_3_), channel_id=1, source_target_pairs={{0,1},{1,0},{2,3},{3,2},{4,5},{5,4},{6,7},{7,6},{8,9},{9,8},{10,11... | collective-permute-start | bytes 1462280 | tf_op jit(solution)/shard_map/ppermute | solution.py:85
  122.0 15.3 %collective-permute-start.27 = (bf16[272,896]{1,0:T(8,128)(2,1)S(1)}, bf16[272,896]{1,0:T(8,128)(2,1)S(1)}, u32[]{:S(2)}, u32[]{:S(2)}) collective-permute-start(bf16[272,896]{1,0:T(8,128)(2,1)S(1)} %collective-permute-done.26.refs_12_.refs_11_), channel_id=1, source_target_pairs={{0,4},{5,1},{4,8},{9,5},{8,12},{13,9},{12,14},{15,13},{14,10},{11,... | collective-permute-start | bytes 1462280 | tf_op jit(solution)/shard_map/ppermute | solution.py:81
  123.5 13.8 %collective-permute-start.24 = (bf16[272,896]{1,0:T(8,128)(2,1)S(1)}, bf16[272,896]{1,0:T(8,128)(2,1)S(1)}, u32[]{:S(2)}, u32[]{:S(2)}) collective-permute-start(bf16[272,896]{1,0:T(8,128)(2,1)S(1)} %collective-permute-done.22.refs_7_.refs_3_), channel_id=1, source_target_pairs={{0,4},{5,1},{4,8},{9,5},{8,12},{13,9},{12,14},{15,13},{14,10},{11,... | collective-permute-start | bytes 1462280 | tf_op jit(solution)/shard_map/ppermute | solution.py:81
  137.3 13.3 %copy-start.6 = (bf16[272,896]{1,0:T(8,128)(2,1)}, bf16[272,896]{1,0:T(8,128)(2,1)S(1)}, u32[]{:S(2)}) copy-start(bf16[272,896]{1,0:T(8,128)(2,1)S(1)} %collective-permute-done.27.refs_7_.refs_13_) | copy-start | bytes 1462276
  137.3 13.2 %copy-start.7 = (bf16[272,896]{1,0:T(8,128)(2,1)}, bf16[272,896]{1,0:T(8,128)(2,1)S(1)}, u32[]{:S(2)}) copy-start(bf16[272,896]{1,0:T(8,128)(2,1)S(1)} %collective-permute-done.24.refs_4_.refs_5_) | copy-start | bytes 1462276
  137.4 8.8 %collective-permute-start.31 = (bf16[272,896]{1,0:T(8,128)(2,1)S(1)}, bf16[272,896]{1,0:T(8,128)(2,1)S(1)}, u32[]{:S(2)}, u32[]{:S(2)}) collective-permute-start(bf16[272,896]{1,0:T(8,128)(2,1)S(1)} %broadcast_select_fusion.9), channel_id=1, source_target_pairs={{0,4},{5,1},{4,8},{9,5},{8,12},{13,9},{12,14},{15,13},{14,10},{11,... | collective-permute-start | bytes 1462280 | tf_op jit(solution)/shard_map/ppermute | solution.py:81
  146.2 2.0 collective-permute-start.32
  146.3 3.2 %collective-permute-start.30 = (bf16[272,896]{1,0:T(8,128)(2,1)S(1)}, bf16[272,896]{1,0:T(8,128)(2,1)S(1)}, u32[]{:S(2)}, u32[]{:S(2)}) collective-permute-start(bf16[272,896]{1,0:T(8,128)(2,1)S(1)} %collective-permute-done.24.refs_4_.refs_5_), channel_id=1, source_target_pairs={{0,1},{1,0},{2,3},{3,2},{4,5},{5,4},{6,7},{7,6},{8,9},{9,8},{10,11... | collective-permute-start | bytes 1462280 | tf_op jit(solution)/shard_map/ppermute | solution.py:85
  147.0 3.6 %collective-permute-start.33 = (bf16[272,896]{1,0:T(8,128)(2,1)S(1)}, bf16[272,896]{1,0:T(8,128)(2,1)S(1)}, u32[]{:S(2)}, u32[]{:S(2)}) collective-permute-start(bf16[272,896]{1,0:T(8,128)(2,1)S(1)} %collective-permute-done.27.refs_7_.refs_13_), channel_id=1, source_target_pairs={{0,1},{1,0},{2,3},{3,2},{4,5},{5,4},{6,7},{7,6},{8,9},{9,8},{10,11... | collective-permute-start | bytes 1462280 | tf_op jit(solution)/shard_map/ppermute | solution.py:85
  166.6 13.5 %copy-start.21 = (bf16[96,7168]{1,0:T(8,128)(2,1)S(1)}, bf16[96,7168]{1,0:T(8,128)(2,1)}, u32[]{:S(2)}) copy-start(bf16[96,7168]{1,0:T(8,128)(2,1)} %get-tuple-element.97) | copy-start | bytes 4128772
  166.6 3.5 %collective-permute-start.35 = (bf16[96,7168]{1,0:T(8,128)(2,1)}, bf16[96,7168]{1,0:T(8,128)(2,1)}, u32[]{:S(2)}, u32[]{:S(2)}) collective-permute-start(bf16[96,7168]{1,0:T(8,128)(2,1)} %get-tuple-element.98), channel_id=1, source_target_pairs={{0,1},{1,0},{2,3},{3,2},{4,5},{5,4},{6,7},{7,6},{8,9},{9,8},{10,11... | collective-permute-start | bytes 4128776 | tf_op jit(solution)/shard_map/ppermute | solution.py:85
  171.6 6.1 %collective-permute-start.36 = (bf16[32,3584]{1,0:T(8,128)(2,1)S(1)}, bf16[32,3584]{1,0:T(8,128)(2,1)S(1)}, u32[]{:S(2)}, u32[]{:S(2)}) collective-permute-start(bf16[32,3584]{1,0:T(8,128)(2,1)S(1)} %get-tuple-element.128), channel_id=1, source_target_pairs={{0,4},{5,1},{4,8},{9,5},{8,12},{13,9},{12,14},{15,13},{14,10},{11,... | collective-permute-start | bytes 688136 | tf_op jit(solution)/shard_map/ppermute | solution.py:81
  173.8 6.3 %collective-permute-start.37 = (bf16[32,3584]{1,0:T(8,128)(2,1)S(1)}, bf16[32,3584]{1,0:T(8,128)(2,1)S(1)}, u32[]{:S(2)}, u32[]{:S(2)}) collective-permute-start(bf16[32,3584]{1,0:T(8,128)(2,1)S(1)} %get-tuple-element.127), channel_id=1, source_target_pairs={{0,4},{5,1},{4,8},{9,5},{8,12},{13,9},{12,14},{15,13},{14,10},{11,... | collective-permute-start | bytes 688136 | tf_op jit(solution)/shard_map/ppermute | solution.py:81
  174.3 15.7 %collective-permute-start.34 = (bf16[160,7168]{1,0:T(8,128)(2,1)}, bf16[160,7168]{1,0:T(8,128)(2,1)S(1)}, u32[]{:S(2)}, u32[]{:S(2)}) collective-permute-start(bf16[160,7168]{1,0:T(8,128)(2,1)} %get-tuple-element.96), channel_id=1, source_target_pairs={{0,1},{1,0},{2,3},{3,2},{4,5},{5,4},{6,7},{7,6},{8,9},{9,8},{10,11... | collective-permute-start | bytes 6881288 | tf_op jit(solution)/shard_map/ppermute | solution.py:85
  181.4 8.5 %collective-permute-start.39 = (bf16[64,3584]{1,0:T(8,128)(2,1)S(1)}, bf16[64,3584]{1,0:T(8,128)(2,1)S(1)}, u32[]{:S(2)}, u32[]{:S(2)}) collective-permute-start(bf16[64,3584]{1,0:T(8,128)(2,1)S(1)} %add_convert_fusion.6), channel_id=1, source_target_pairs={{0,4},{5,1},{4,8},{9,5},{8,12},{13,9},{12,14},{15,13},{14,10},{11,... | collective-permute-start | bytes 1376264 | tf_op jit(solution)/shard_map/ppermute | solution.py:81
  184.9 10.0 %collective-permute-start.38 = (bf16[64,3584]{1,0:T(8,128)(2,1)S(1)}, bf16[64,3584]{1,0:T(8,128)(2,1)S(1)}, u32[]{:S(2)}, u32[]{:S(2)}) collective-permute-start(bf16[64,3584]{1,0:T(8,128)(2,1)S(1)} %add_convert_fusion.5), channel_id=1, source_target_pairs={{0,4},{5,1},{4,8},{9,5},{8,12},{13,9},{12,14},{15,13},{14,10},{11,... | collective-permute-start | bytes 1376264 | tf_op jit(solution)/shard_map/ppermute | solution.py:81
  190.1 9.6 %collective-permute-start.41 = (bf16[64,3584]{1,0:T(8,128)(2,1)S(1)}, bf16[64,3584]{1,0:T(8,128)(2,1)S(1)}, u32[]{:S(2)}, u32[]{:S(2)}) collective-permute-start(bf16[64,3584]{1,0:T(8,128)(2,1)S(1)} %add_convert_fusion.4), channel_id=1, source_target_pairs={{0,4},{5,1},{4,8},{9,5},{8,12},{13,9},{12,14},{15,13},{14,10},{11,... | collective-permute-start | bytes 1376264 | tf_op jit(solution)/shard_map/ppermute | solution.py:81
  195.0 9.7 %collective-permute-start.40 = (bf16[64,3584]{1,0:T(8,128)(2,1)S(1)}, bf16[64,3584]{1,0:T(8,128)(2,1)S(1)}, u32[]{:S(2)}, u32[]{:S(2)}) collective-permute-start(bf16[64,3584]{1,0:T(8,128)(2,1)S(1)} %add_convert_fusion.3), channel_id=1, source_target_pairs={{0,4},{5,1},{4,8},{9,5},{8,12},{13,9},{12,14},{15,13},{14,10},{11,... | collective-permute-start | bytes 1376264 | tf_op jit(solution)/shard_map/ppermute | solution.py:81
  200.0 9.6 %collective-permute-start.42 = (bf16[64,3584]{1,0:T(8,128)(2,1)S(1)}, bf16[64,3584]{1,0:T(8,128)(2,1)S(1)}, u32[]{:S(2)}, u32[]{:S(2)}) collective-permute-start(bf16[64,3584]{1,0:T(8,128)(2,1)S(1)} %add_convert_fusion.2), channel_id=1, source_target_pairs={{0,4},{5,1},{4,8},{9,5},{8,12},{13,9},{12,14},{15,13},{14,10},{11,... | collective-permute-start | bytes 1376264 | tf_op jit(solution)/shard_map/ppermute | solution.py:81
  209.6 2.5 %collective-permute-start.43 = (bf16[32,3584]{1,0:T(8,128)(2,1)S(1)}, bf16[32,3584]{1,0:T(8,128)(2,1)S(1)}, u32[]{:S(2)}, u32[]{:S(2)}) collective-permute-start(bf16[32,3584]{1,0:T(8,128)(2,1)S(1)} %broadcast_select_fusion.11), channel_id=1, source_target_pairs={{0,1},{1,0},{2,3},{3,2},{4,5},{5,4},{6,7},{7,6},{8,9},{9,8},{10,11... | collective-permute-start | bytes 688136 | tf_op jit(solution)/shard_map/ppermute | solution.py:85
  209.7 11.8 %copy-start.1 = (bf16[32,64,576]{2,1,0:T(8,128)(2,1)S(1)}, bf16[32,64,576]{2,1,0:T(8,128)(2,1)}, u32[]{:S(2)}) copy-start(bf16[32,64,576]{2,1,0:T(8,128)(2,1)} %param.13) | copy-start | bytes 7077892
  209.9 8.5 %collective-permute-start.45 = (bf16[64,3584]{1,0:T(8,128)(2,1)S(1)}, bf16[64,3584]{1,0:T(8,128)(2,1)S(1)}, u32[]{:S(2)}, u32[]{:S(2)}) collective-permute-start(bf16[64,3584]{1,0:T(8,128)(2,1)S(1)} %add_convert_fusion.1), channel_id=1, source_target_pairs={{0,4},{5,1},{4,8},{9,5},{8,12},{13,9},{12,14},{15,13},{14,10},{11,... | collective-permute-start | bytes 1376264 | tf_op jit(solution)/shard_map/ppermute | solution.py:81
  212.3 6.8 %collective-permute-start.44 = (bf16[32,3584]{1,0:T(8,128)(2,1)S(1)}, bf16[32,3584]{1,0:T(8,128)(2,1)S(1)}, u32[]{:S(2)}, u32[]{:S(2)}) collective-permute-start(bf16[32,3584]{1,0:T(8,128)(2,1)S(1)} %add_convert_fusion.8), channel_id=1, source_target_pairs={{0,16},{16,0},{1,17},{17,1},{2,18},{18,2},{3,19},{19,3},{4,20},{20... | collective-permute-start | bytes 688136 | tf_op jit(solution)/shard_map/ppermute | solution.py:184
  219.1 1.6 collective-permute-start.46
  (20 other events, 60.6 us)
where the time goes:
time: 223 us; the launch traced here: 222 us
  waiting for transfers between devices  78.9 us (35%)
  starting transfers between devices  48.7 us (22%)
  Pallas kernels  42.6 us (19%)
  local copies, waits for them, and re-layouts  19.9 us (9%)
  other arithmetic  18.7 us (8%)
  matrix products  12 us (5%)
    ppermute x22, waiting for transfers between devices, ring_step(): return lax.ppermute(block, ('chip', 'core'), pairs)  64.8 us
    ppermute x22, starting transfers between devices, ring_step(): return lax.ppermute(block, ('chip', 'core'), pairs)  36.1 us
    pallas_call x1, Pallas kernels, tail(): pl.pallas_call(functools.partial(tail_kernel, len(gate_up), first, count,...  14.2 us
    pallas_call x2, Pallas kernels, project(): pl.pallas_call(functools.partial(project_kernel, steps, ahead, count), ou...  14 us
    unnamed x68, local copies, waits for them, and re-layouts  13.8 us
    pallas_call x1, Pallas kernels, gate(): pl.pallas_call(functools.partial(gate_kernel, len(gate_up), first, count,...  10.5 us
    ppermute x22, waiting for transfers between devices, swap_cores(): return lax.ppermute(block, 'core', SWAP)  9.22 us
    all_to_all x1, starting transfers between devices, body(): lax.all_to_all(jnp.concatenate([outgoing, names], axis=2), 'chip', split_...  7.29 us
  transfers between devices with their start and end apart: 48, of which 30 were waited for; matrix products, arithmetic and copies ran while one was open for 17% of the time, Pallas kernels for 12%

commit v1 on v0

--- a/solution.py
+++ b/solution.py
@@ -96,6 +96,8 @@
     for i in range(chips // 2 - 1):
         for s in range(STREAMS):
             moving[s] = ring_step(between(s, i, moving[s], pieces))
+            if 0 < i < chips // 2 - 2:
+                moving[s], pieces[s][-1] = lax.optimization_barrier((moving[s], pieces[s][-1]))
             if i < chips // 2 - 2:
                 pieces[s] += [moving[s], swap_cores(moving[s])]
     moving = between(STREAMS - 1, None, moving, pieces)
@@ -176,8 +178,7 @@
         at += 2 * rows
     sums = []
     for s in range(STREAMS):
-        if sums:
-            moving[s], _ = lax.optimization_barrier((moving[s], sums[0]))
+        moving[s], _ = lax.optimization_barrier((moving[s], sums[0] if sums else ahead))
         mine, theirs = by_core(core, moving[s][:rows], moving[s][rows:])
         added = plus(cut(at, rows, s), plus(mine, swap_cores(theirs)))
         if groups == STREAMS and s == 0:
@@ -200,9 +201,8 @@
     return ready
 
 
-def project_kernel(steps, ahead, count, weight, *refs):
-    pieces, (out, rows, held, turned, piece_sems, weight_sems) = refs[:-6], refs[-6:]
-    few = out.shape[0] <= 128
+def project_kernel(steps, count, weight, *refs):
+    pieces, (out, rows, held, piece_sems, weight_sems) = refs[:-5], refs[-5:]
     depth = held.shape[2]
     block, half = pieces[0].shape
     copies = []
@@ -215,48 +215,87 @@
 
     def weight_copy(k):
         columns = pl.ds(pl.multiple_of(k * depth, depth), depth)
-        slot = k % (ahead + 1)
+        slot = k % 3
         return pltpu.make_async_copy(weight.at[:, columns], held.at[slot], weight_sems.at[slot])
 
-    ready = stream(steps, ahead, weight_copy)
+    ready = stream(steps, 2, weight_copy)
     for copy in copies:
         copy.wait()
-    total = turned if few else out
-    total[...] = jnp.zeros_like(total)
+    out[...] = jnp.zeros_like(out)
 
     @pl.loop(0, steps)
     def _(k):
         ready(k)
         columns = pl.ds(pl.multiple_of(k * depth, depth), depth)
-        left, right = rows[:, columns], held[k % (ahead + 1)]
-        if few:
-            left, right = right, left
-        total[...] += lax.dot_general(left, right, NT, preferred_element_type=jnp.float32)
-
-    if few:
-        out[...] = turned[...].T
-
-
-def project(pieces, weight, ahead, grant):
+        out[...] += lax.dot_general(
+            rows[:, columns], held[k % 3], NT, preferred_element_type=jnp.float32
+        )
+
+
+def project_few_kernel(steps, weight, *refs):
+    pieces, (out, rows, held, turned, piece_sems, weight_sems) = refs[:-6], refs[-6:]
+    half = pieces[0].shape[1]
+    parts = weight_sems.shape[0]
+    size = held.shape[0] // parts
+    copies = []
+    for p in range(parts):
+        span = pl.ds(p * size, size)
+        copies.append(
+            pltpu.make_async_copy(weight.at[span, :], held.at[span, :], weight_sems.at[p])
+        )
+    for s, piece in enumerate(pieces):
+        target = rows.at[:, pl.ds(s * half, half)]
+        copies.append(pltpu.make_async_copy(piece, target, piece_sems.at[s]))
+    for copy in copies:
+        copy.start()
+    for copy in copies:
+        copy.wait()
+    turned[...] = jnp.zeros_like(turned)
+    depth = rows.shape[1] // steps
+
+    @pl.loop(0, steps)
+    def _(k):
+        columns = pl.ds(pl.multiple_of(k * depth, depth), depth)
+        turned[...] += lax.dot_general(
+            held[:, columns], rows[:, columns], NT, preferred_element_type=jnp.float32
+        )
+
+    out[...] = turned[...].T
+
+
+def project(pieces, weight):
     count = len(pieces[0])
     rows, half = pieces[0][0].shape
     depth = STREAMS * half
     columns = weight.shape[0]
     steps = 8
     total = count * rows
+    few = count == 1
+    if few:
+        kernel = functools.partial(project_few_kernel, steps)
+        held = [
+            pltpu.VMEM((columns, depth), jnp.bfloat16),
+            pltpu.VMEM((columns, total), jnp.float32),
+        ]
+        weight_sems = 2
+    else:
+        kernel = functools.partial(project_kernel, steps, count)
+        held = [pltpu.VMEM((3, columns, depth // steps), jnp.bfloat16)]
+        weight_sems = 3
     return pl.pallas_call(
-        functools.partial(project_kernel, steps, ahead, count),
+        kernel,
         out_shape=jax.ShapeDtypeStruct((total, columns), jnp.float32),
         in_specs=[ANY] * (1 + STREAMS * count),
         out_specs=IN_VMEM,
-        scratch_shapes=[
-            pltpu.VMEM((total, depth), jnp.bfloat16),
-            pltpu.VMEM((ahead + 1, columns, depth // steps), jnp.bfloat16),
-            pltpu.VMEM((columns, total) if total <= 128 else (8, 128), jnp.float32),
+        scratch_shapes=[pltpu.VMEM((total, depth), jnp.bfloat16)]
+        + held
+        + [
             pltpu.SemaphoreType.DMA((STREAMS * count,)),
-            pltpu.SemaphoreType.DMA((ahead + 1,)),
+            pltpu.SemaphoreType.DMA((weight_sems,)),
         ],
-        compiler_params=pltpu.CompilerParams(vmem_limit_bytes=grant),
+        compiler_params=pltpu.CompilerParams(
+            vmem_limit_bytes=VMEM if few else 20 * 1024 * 1024
+        ),
         cost_estimate=pl.CostEstimate(
             flops=2 * total * depth * columns,
             bytes_accessed=2 * depth * (total + columns) + 4 * total * columns,
@@ -438,7 +477,8 @@
     rows = held.shape[1]
     depth = pieces[0].shape[1]
     hidden = active.shape[1]
-    steps, _, span = second.shape
+    span = staged.shape[2]
+    steps = second.shape[1] // span
     for k in range(count):
         side = held.shape[2] // depth
         target = weight.at[k // side, pl.ds(k % side * depth, depth), :]
@@ -450,9 +490,15 @@
     def columns(n):
         return pl.ds(pl.multiple_of(n * span, span), span)
 
-    @pl.loop(0, steps)
-    def _(n):
-        pltpu.make_async_copy(down.at[:, columns(n)], second.at[n], second_sems.at[n]).start()
+    def second_copy(n):
+        size = hidden // second_sems.shape[0]
+        span_rows = pl.ds(n * size, size)
+        return pltpu.make_async_copy(
+            down.at[span_rows, :], second.at[span_rows, :], second_sems.at[n]
+        )
+
+    for n in range(second_sems.shape[0]):
+        second_copy(n).start()
 
     add_products(count, depth, held, weight, total, piece_sems, weight_sems)
 
@@ -466,6 +512,9 @@
     for i in range(2 * chips):
         at = pl.ds(pl.multiple_of(meta[chips + 1 + i] * share, share), share)
         ordered[i * share : (i + 1) * share, :] = active[at, :]
+
+    for n in range(second_sems.shape[0]):
+        second_copy(n).wait()
 
     def out_copies(n):
         copies, at = [], 0
@@ -481,14 +530,14 @@
 
     @pl.loop(0, steps)
     def _(n):
-        pltpu.make_async_copy(down.at[:, columns(n)], second.at[n], second_sems.at[n]).wait()
-
         @pl.when(n >= 2)
         def _():
             for copy in out_copies(n - 2):
                 copy.wait()
 
-        result = jnp.dot(ordered[...], second[n], preferred_element_type=jnp.float32)
+        result = jnp.dot(
+            ordered[...], second[:, columns(n)], preferred_element_type=jnp.float32
+        )
         staged[n % 2] = result.astype(jnp.bfloat16)
         for copy in out_copies(n):
             copy.start()
@@ -521,12 +570,12 @@
             pltpu.VMEM((rows, wide), jnp.float32),
             pltpu.VMEM((rows, hidden), jnp.bfloat16),
             pltpu.VMEM((rows, hidden), jnp.bfloat16),
-            pltpu.VMEM((steps, hidden, width // steps), jnp.bfloat16),
+            pltpu.VMEM((hidden, width), jnp.bfloat16),
             pltpu.VMEM((2, rows, width // steps), jnp.bfloat16),
             pltpu.SemaphoreType.DMA((count,)),
             pltpu.SemaphoreType.DMA((count,)),
             pltpu.SemaphoreType.DMA(()),
-            pltpu.SemaphoreType.DMA((steps,)),
+            pltpu.SemaphoreType.DMA((4,)),
             pltpu.SemaphoreType.DMA((2, 4)),
         ],
         compiler_params=pltpu.CompilerParams(vmem_limit_bytes=VMEM),
@@ -574,26 +623,27 @@
     )
 
     parts = 4
-    span = width // parts
+    quarter_rows = width // parts
     gate_up = []
-    stages = [None, (0, 0), (1, 0), (0, 1)]
     final = chips // 2 - 1
-    ends = [(1, 1), (0, 2), (1, 2), (None, final)]
     projected = []
+
+    def quarter(moving, after):
+        p = len(gate_up)
+        raw, _ = lax.optimization_barrier((w_gate_up, after))
+        part = raw[0, p * quarter_rows : (p + 1) * quarter_rows].reshape(quarter_rows, -1)
+        moving, part = lax.optimization_barrier((moving, part))
+        gate_up.append(part)
+        return moving
 
     def during_first(s, i, moving, pieces):
         if (s, i) == (None, None):
-            part = project([piece[: chips - 1] for piece in pieces], out_proj.T, 2, 20 * 1024 * 1024)
+            part = project([piece[: chips - 1] for piece in pieces], out_proj.T)
             moving, part = lax.optimization_barrier((moving, part))
             projected.append(part)
-        if (s, i) in ends:
-            p = ends.index((s, i))
-            raw = w_gate_up
-            if stages[p] is not None:
-                raw, _ = lax.optimization_barrier((raw, pieces[stages[p][0]][1 + 2 * stages[p][1]]))
-            quarter = raw[0, p * span : (p + 1) * span].reshape(span, -1)
-            moving, quarter = lax.optimization_barrier((moving, quarter))
-            gate_up.append(quarter)
+        if (s, i) == (1, 1):
+            for t in range(STREAMS):
+                moving = quarter(moving, pieces[t][0])
         return moving
 
     own_gain = lax.dynamic_slice_in_dim(norm_gain, place * own_cols, own_cols, 0)[None]
@@ -608,7 +658,7 @@
     block = jnp.concatenate([low, high], axis=0)
     half = block.shape[1] // STREAMS
     pieces = ring_gather([block[:, s * half : (s + 1) * half] for s in range(STREAMS)], during_first)
-    projected.append(project([piece[chips - 1 :] for piece in pieces], out_proj.T, 8, VMEM))
+    projected.append(project([piece[chips - 1 :] for piece in pieces], out_proj.T))
     parts, got = [], []
     for part in projected:
         if groups == 2:
@@ -658,6 +708,9 @@
     def during_second(s, i, moving, pieces):
         if (s, i) == (STREAMS - 1, None):
             moving, sums[0] = lax.optimization_barrier((moving, sums[0]))
+        if (s, i) == (1, 1):
+            for t in range(STREAMS):
+                moving = quarter(moving, pieces[t][0])
         if (s, i) == (STREAMS - 1, final - 1):
             blocks = [piece[: chips - 3] for piece in pieces]
             blocks, _ = lax.optimization_barrier((blocks, moving))

time: 223 us -> 223 us (level)
  transfers between devices with their start and end apart: 48 -> 48, of which waited for: 30 -> 28; matrix products, arithmetic and copies ran while one was open for 17% -> 17% of each run, Pallas kernels for 12% -> 12%
where the time goes in v1:
time: 223 us; the launch traced here: 222 us
  waiting for transfers between devices  78.3 us (35%)
  starting transfers between devices  48.9 us (22%)
  Pallas kernels  43.2 us (19%)
  local copies, waits for them, and re-layouts  19.8 us (9%)
  other arithmetic  18.7 us (8%)
  matrix products  12 us (5%)
    ppermute x22, waiting for transfers between devices, ring_step(): return lax.ppermute(block, ('chip', 'core'), pairs)  64.2 us
    ppermute x22, starting transfers between devices, ring_step(): return lax.ppermute(block, ('chip', 'core'), pairs)  36.5 us
    pallas_call x1, Pallas kernels, tail(): pl.pallas_call(functools.partial(tail_kernel, len(gate_up), first, count,...  14.7 us
    pallas_call x2, Pallas kernels, project(): pl.pallas_call(kernel, out_shape=jax.ShapeDtypeStruct((total, columns), j...  14.1 us
    unnamed x68, local copies, waits for them, and re-layouts  13.6 us
    pallas_call x1, Pallas kernels, gate(): pl.pallas_call(functools.partial(gate_kernel, len(gate_up), first, count,...  10.5 us
    ppermute x22, waiting for transfers between devices, swap_cores(): return lax.ppermute(block, 'core', SWAP)  9.13 us
    all_to_all x1, starting transfers between devices, body(): lax.all_to_all(jnp.concatenate([outgoing, names], axis=2), 'chip', split_...  7.29 us
  transfers between devices with their start and end apart: 48, of which 28 were waited for; matrix products, arithmetic and copies ran while one was open for 17% of the time, Pallas kernels for 12%

profile of v1, /device:TPU:0, one launch (start us, length us, event | category | flops | bytes accessed | tf_op | source)
XLA Modules:
  0.0 221.7 jit_solution(14257496443779361491)
XLA Ops:
  0.0 1.2 copy.56
  2.9 7.3 %all-to-all-start = ((bf16[8,32,904]{2,1,0:T(8,128)(2,1)}), bf16[8,32,904]{2,1,0:T(8,128)(2,1)S(1)}, u32[]{:S(2)}, u32[]{:S(2)}) async-start(bf16[8,32,904]{2,1,0:T(8,128)(2,1)} %pad_maximum_fusion.2), calls=%async_computation | async-start | bytes 1048576 | tf_op jit(solution)/shard_map/all_to_all | solution.py:621
  11.2 6.7 %fusion.6 = (f32[32,64]{1,0:T(8,128)S(1)}, f32[32,64,192]{2,1,0:T(8,128)S(1)}) fusion(pred[32,192]{1,0:T(8,128)(4,1)S(1)} %iota_compare_fusion.1, bf16[32,64,576]{2,1,0:T(8,128)(2,1)S(1)} %copy-done, bf16[32,192,576]{2,1,0:T(8,128)(2,1)} %param.14), kind=kOutput, calls=%fused_computation.8 | convolution fusion | flops 454162432 | bytes 11024384 | tf_op jit(solution)/shard_map/thk,tjk->thj/dot_general | solution.py:33
  19.0 2.0 add_convert_fusion
  21.7 2.3 %fusion.11 = bf16[64,4,8,128]{3,2,1,0:T(8,128)(2,1)S(1)} fusion(bf16[64,512,128]{2,1,0:T(8,128)(2,1)S(1)} %bitcast.115, bf16[32,64,512]{2,1,0:T(8,128)(2,1)S(1)} %add_convert_fusion), kind=kOutput, calls=%fused_computation.11 | convolution fusion | flops 268697600 | bytes 11010048 | tf_op jit(solution)/shard_map/thc,hcd->thd/dot_general | solution.py:59
  24.7 1.9 collective-permute-done.1
  26.7 1.6 collective-permute-start.6
  28.3 1.5 collective-permute-start.2
  30.4 2.8 %copy.41 = bf16[224,8,2,512]{3,1,2,0:T(8,128)(2,1)} copy(bf16[224,8,2,512]{3,2,1,0:T(2,128)(2,1)S(1)} %bitcast.116) | data formatting | bytes 7340032
  33.2 2.9 %copy.42 = bf16[224,8,2,512]{3,1,2,0:T(8,128)(2,1)} copy(bf16[224,8,2,512]{3,2,1,0:T(2,128)(2,1)S(1)} %bitcast.117) | data formatting | bytes 7340032
  36.1 1.5 collective-permute-start.7
  37.6 4.0 %collective-permute-done.2.refs_1_ = bf16[64,4096]{1,0:T(8,128)(2,1)S(1)} collective-permute-done((bf16[64,4096]{1,0:T(8,128)(2,1)S(1)}, bf16[64,4096]{1,0:T(8,128)(2,1)S(1)}, u32[]{:S(2)}, u32[]{:S(2)}) %collective-permute-start.2) | collective-permute-done | bytes 524320 | tf_op jit(solution)/shard_map/ppermute | solution.py:81
  41.6 1.5 collective-permute-start.3
  43.1 4.1 %collective-permute-done.7.refs_10_ = bf16[64,4096]{1,0:T(8,128)(2,1)S(1)} collective-permute-done((bf16[64,4096]{1,0:T(8,128)(2,1)S(1)}, bf16[64,4096]{1,0:T(8,128)(2,1)S(1)}, u32[]{:S(2)}, u32[]{:S(2)}) %collective-permute-start.7) | collective-permute-done | bytes 524320 | tf_op jit(solution)/shard_map/ppermute | solution.py:81
  47.2 1.5 collective-permute-start.9
  48.8 4.1 %collective-permute-done.3.refs_3_ = bf16[64,4096]{1,0:T(8,128)(2,1)S(1)} collective-permute-done((bf16[64,4096]{1,0:T(8,128)(2,1)S(1)}, bf16[64,4096]{1,0:T(8,128)(2,1)S(1)}, u32[]{:S(2)}, u32[]{:S(2)}) %collective-permute-start.3) | collective-permute-done | bytes 524320 | tf_op jit(solution)/shard_map/ppermute | solution.py:81
  52.8 1.5 collective-permute-start.5
  54.9 3.6 %collective-permute-done.9.refs_12_ = bf16[64,4096]{1,0:T(8,128)(2,1)S(1)} collective-permute-done((bf16[64,4096]{1,0:T(8,128)(2,1)S(1)}, bf16[64,4096]{1,0:T(8,128)(2,1)S(1)}, u32[]{:S(2)}, u32[]{:S(2)}) %collective-permute-start.9) | collective-permute-done | bytes 524320 | tf_op jit(solution)/shard_map/ppermute | solution.py:81
  58.4 5.6 %collective-permute-done.5.refs_5_ = bf16[64,4096]{1,0:T(8,128)(2,1)S(1)} collective-permute-done((bf16[64,4096]{1,0:T(8,128)(2,1)S(1)}, bf16[64,4096]{1,0:T(8,128)(2,1)S(1)}, u32[]{:S(2)}, u32[]{:S(2)}) %collective-permute-start.5) | collective-permute-done | bytes 524320 | tf_op jit(solution)/shard_map/ppermute | solution.py:81
  64.1 1.8 collective-permute-start.10
  66.2 6.9 %shard_map.118.refs_0_ = f32[448,448]{1,0:T(8,128)S(1)} custom-call(bf16[448,8192]{1,0:T(8,128)(2,1)S(1)} %bitcast.100, bf16[64,4096]{1,0:T(8,128)(2,1)S(1)} %get-tuple-element.154.refs_0_, bf16[64,4096]{1,0:T(8,128)(2,1)S(1)} %collective-permute-done.2.refs_1_, bf16[64,4096]{1,0:T(8,128)(2,1)S(1)} %collective-permute-done.4.refs_2_, ...), custom_call_target="tpu_custom_call" | custom-call | flops 3288334336 | bytes 15482880 | tf_op jit(solution)/shard_map/pallas_call | solution.py:285
  74.7 1.1 select_bitcast_fusion.1
  75.8 1.6 collective-permute-start.16
  77.4 2.1 broadcast_select_fusion.4
  79.5 7.2 %shard_map.119.refs_1_ = f32[64,448]{1,0:T(8,128)} custom-call(bf16[448,8192]{1,0:T(8,128)(2,1)} %bitcast.97, bf16[64,4096]{1,0:T(8,128)(2,1)} %get-tuple-element.152.refs_0_, bf16[64,4096]{1,0:T(8,128)(2,1)} %get-tuple-element.151.refs_1_), custom_call_target="tpu_custom_call" | custom-call | flops 469762048 | bytes 8503296 | tf_op jit(solution)/shard_map/pallas_call | solution.py:285
  88.8 3.2 %collective-permute-done.17.refs_3_ = bf16[64,448]{1,0:T(8,128)(2,1)S(1)} collective-permute-done((bf16[64,448]{1,0:T(8,128)(2,1)S(1)}, bf16[64,448]{1,0:T(8,128)(2,1)S(1)}, u32[]{:S(2)}, u32[]{:S(2)}) %collective-permute-start.17) | collective-permute-done | bytes 57376 | tf_op jit(solution)/shard_map/ppermute | solution.py:666
  92.0 1.3 shard_map.120
  96.0 1.6 collective-permute-start.25
  97.6 1.6 collective-permute-start.20
  99.8 2.8 %copy.43 = bf16[224,8,2,512]{3,1,2,0:T(8,128)(2,1)} copy(bf16[224,8,2,512]{3,2,1,0:T(2,128)(2,1)S(1)} %bitcast.118) | data formatting | bytes 7340032
  102.6 2.0 slice-done.7
  104.7 2.8 %copy.44 = bf16[224,8,2,512]{3,1,2,0:T(8,128)(2,1)} copy(bf16[224,8,2,512]{3,2,1,0:T(2,128)(2,1)S(1)} %bitcast.119) | data formatting | bytes 7340032
  107.5 1.5 collective-permute-start.26
  110.0 1.5 collective-permute-start.21
  111.6 4.7 %collective-permute-done.26.refs_12_.refs_11_ = bf16[272,896]{1,0:T(8,128)(2,1)S(1)} collective-permute-done((bf16[272,896]{1,0:T(8,128)(2,1)S(1)}, bf16[272,896]{1,0:T(8,128)(2,1)S(1)}, u32[]{:S(2)}, u32[]{:S(2)}) %collective-permute-start.26) | collective-permute-done | bytes 487456 | tf_op jit(solution)/shard_map/ppermute | solution.py:81
  116.4 5.1 %collective-permute-done.21.refs_7_.refs_3_ = bf16[272,896]{1,0:T(8,128)(2,1)S(1)} collective-permute-done((bf16[272,896]{1,0:T(8,128)(2,1)S(1)}, bf16[272,896]{1,0:T(8,128)(2,1)S(1)}, u32[]{:S(2)}, u32[]{:S(2)}) %collective-permute-start.21) | collective-permute-done | bytes 487456 | tf_op jit(solution)/shard_map/ppermute | solution.py:81
  121.6 1.6 collective-permute-start.28
  123.1 1.4 collective-permute-start.24
  126.2 10.5 %shard_map.121.before = f32[512,1024]{1,0:T(8,128)} custom-call(s32[25]{0:T(128)} %copy-done.3, bf16[1792,1024]{1,0:T(8,128)(2,1)} %bitcast.106, bf16[1792,1024]{1,0:T(8,128)(2,1)} %bitcast.108, bf16[1792,1024]{1,0:T(8,128)(2,1)} %bitcast.110, bf16[1792,1024]{1,0:T(8,128)(2,1)} %bitcast.112, bf16[272,896]{1,0:T(8,128)(2,1)} %copy-done.9, ...), custom_call_target="tpu_custom_call" | custom-call | flops 4697620480 | bytes 13762560 | tf_op jit(solution)/shard_map/pallas_call | solution.py:451
  136.8 2.4 %collective-permute-start.31 = (bf16[272,896]{1,0:T(8,128)(2,1)S(1)}, bf16[272,896]{1,0:T(8,128)(2,1)S(1)}, u32[]{:S(2)}, u32[]{:S(2)}) collective-permute-start(bf16[272,896]{1,0:T(8,128)(2,1)S(1)} %broadcast_select_fusion.9), channel_id=1, source_target_pairs={{0,4},{5,1},{4,8},{9,5},{8,12},{13,9},{12,14},{15,13},{14,10},{11,... | collective-permute-start | bytes 1462280 | tf_op jit(solution)/shard_map/ppermute | solution.py:81
  139.2 6.7 %collective-permute-done.31 = bf16[272,896]{1,0:T(8,128)(2,1)S(1)} collective-permute-done((bf16[272,896]{1,0:T(8,128)(2,1)S(1)}, bf16[272,896]{1,0:T(8,128)(2,1)S(1)}, u32[]{:S(2)}, u32[]{:S(2)}) %collective-permute-start.31) | collective-permute-done | bytes 487456 | tf_op jit(solution)/shard_map/ppermute | solution.py:81
  146.8 1.1 collective-permute-done.32
  147.9 1.3 broadcast_select_fusion.8
  152.1 14.7 %shard_map.122 = (bf16[96,7168]{1,0:T(8,128)(2,1)}, bf16[96,7168]{1,0:T(8,128)(2,1)}, bf16[160,7168]{1,0:T(8,128)(2,1)}, bf16[160,7168]{1,0:T(8,128)(2,1)}) custom-call(s32[25]{0:T(128)} %copy-done.3, f32[2,512]{1,0:T(2,128)} %pad_maximum_fusion.9.factors, f32[512,1024]{1,0:T(8,128)} %shard_map.121.before, bf16[512,7168]{1,0:T(8,128)(2,1)} %bitcast.122, ...), custom_call_target="tpu_custom_call" | custom-call | flops 6576668672 | bytes 22937600 | tf_op jit(solution)/shard_map/pallas_call | solution.py:559
  167.0 3.3 %collective-permute-done.35 = bf16[96,7168]{1,0:T(8,128)(2,1)} collective-permute-done((bf16[96,7168]{1,0:T(8,128)(2,1)}, bf16[96,7168]{1,0:T(8,128)(2,1)}, u32[]{:S(2)}, u32[]{:S(2)}) %collective-permute-start.35) | collective-permute-done | bytes 1376288 | tf_op jit(solution)/shard_map/ppermute | solution.py:85
  170.3 1.4 add_convert_fusion.9
  171.7 2.2 collective-permute-start.36
  174.4 3.4 %collective-permute-done.36 = bf16[32,3584]{1,0:T(8,128)(2,1)S(1)} collective-permute-done((bf16[32,3584]{1,0:T(8,128)(2,1)S(1)}, bf16[32,3584]{1,0:T(8,128)(2,1)S(1)}, u32[]{:S(2)}, u32[]{:S(2)}) %collective-permute-start.36) | collective-permute-done | bytes 229408 | tf_op jit(solution)/shard_map/ppermute | solution.py:81
  177.8 2.5 %collective-permute-done.37 = bf16[32,3584]{1,0:T(8,128)(2,1)S(1)} collective-permute-done((bf16[32,3584]{1,0:T(8,128)(2,1)S(1)}, bf16[32,3584]{1,0:T(8,128)(2,1)S(1)}, u32[]{:S(2)}, u32[]{:S(2)}) %collective-permute-start.37) | collective-permute-done | bytes 229408 | tf_op jit(solution)/shard_map/ppermute | solution.py:81
  180.3 1.2 add_convert_fusion.6
  181.6 2.2 collective-permute-start.39
  183.8 1.2 add_convert_fusion.5
  185.5 2.5 %shard_map.123 = bf16[8,32,896]{2,1,0:T(8,128)(2,1)} custom-call(s32[25]{0:T(128)} %copy-done.3, bf16[272,896]{1,0:T(8,128)(2,1)} %copy-done.9, bf16[272,896]{1,0:T(8,128)(2,1)} %copy-done.12, bf16[272,896]{1,0:T(8,128)(2,1)} %copy-done.16, bf16[272,896]{1,0:T(8,128)(2,1)} %copy-done.15, bf16[272,896]{1,0:T(8,128)(2,1)} %copy-done.18, ...), custom_call_target="tpu_custom_call" | custom-call | tf_op jit(solution)/shard_map/pallas_call | solution.py:367
  188.0 1.1 convert_bitcast_fusion
  190.3 2.2 collective-permute-start.41
  192.5 2.6 %collective-permute-done.38 = bf16[64,3584]{1,0:T(8,128)(2,1)S(1)} collective-permute-done((bf16[64,3584]{1,0:T(8,128)(2,1)S(1)}, bf16[64,3584]{1,0:T(8,128)(2,1)S(1)}, u32[]{:S(2)}, u32[]{:S(2)}) %collective-permute-start.38) | collective-permute-done | bytes 458784 | tf_op jit(solution)/shard_map/ppermute | solution.py:81
  195.2 2.2 collective-permute-start.40
  197.4 2.6 %collective-permute-done.41 = bf16[64,3584]{1,0:T(8,128)(2,1)S(1)} collective-permute-done((bf16[64,3584]{1,0:T(8,128)(2,1)S(1)}, bf16[64,3584]{1,0:T(8,128)(2,1)S(1)}, u32[]{:S(2)}, u32[]{:S(2)}) %collective-permute-start.41) | collective-permute-done | bytes 458784 | tf_op jit(solution)/shard_map/ppermute | solution.py:81
  200.1 2.2 collective-permute-start.42
  202.3 2.6 %collective-permute-done.40 = bf16[64,3584]{1,0:T(8,128)(2,1)S(1)} collective-permute-done((bf16[64,3584]{1,0:T(8,128)(2,1)S(1)}, bf16[64,3584]{1,0:T(8,128)(2,1)S(1)}, u32[]{:S(2)}, u32[]{:S(2)}) %collective-permute-start.40) | collective-permute-done | bytes 458784 | tf_op jit(solution)/shard_map/ppermute | solution.py:81
  205.0 4.7 %collective-permute-done.42 = bf16[64,3584]{1,0:T(8,128)(2,1)S(1)} collective-permute-done((bf16[64,3584]{1,0:T(8,128)(2,1)S(1)}, bf16[64,3584]{1,0:T(8,128)(2,1)S(1)}, u32[]{:S(2)}, u32[]{:S(2)}) %collective-permute-start.42) | collective-permute-done | bytes 458784 | tf_op jit(solution)/shard_map/ppermute | solution.py:81
  209.9 2.2 collective-permute-start.45
  212.8 5.6 %collective-permute-done.45 = bf16[64,3584]{1,0:T(8,128)(2,1)S(1)} collective-permute-done((bf16[64,3584]{1,0:T(8,128)(2,1)S(1)}, bf16[64,3584]{1,0:T(8,128)(2,1)S(1)}, u32[]{:S(2)}, u32[]{:S(2)}) %collective-permute-start.45) | collective-permute-done | bytes 458784 | tf_op jit(solution)/shard_map/ppermute | solution.py:81
  219.3 1.5 collective-permute-done.46
  (196 shorter events, 25.6 us)
Async XLA Ops:
  0.0 10.3 %copy-start = (bf16[32,64,576]{2,1,0:T(8,128)(2,1)S(1)}, bf16[32,64,576]{2,1,0:T(8,128)(2,1)}, u32[]{:S(2)}) copy-start(bf16[32,64,576]{2,1,0:T(8,128)(2,1)} %param.13) | copy-start | bytes 7077892
  0.0 10.2 %copy-start.25 = (s32[32]{0:T(128)S(1)}, s32[32]{0:T(128)}, u32[]{:S(2)}) copy-start(s32[32]{0:T(128)} %param.16) | copy-start | bytes 388
  0.0 10.2 %copy-start.23 = (bf16[32,576]{1,0:T(8,128)(2,1)S(1)}, bf16[32,576]{1,0:T(8,128)(2,1)}, u32[]{:S(2)}) copy-start(bf16[32,576]{1,0:T(8,128)(2,1)} %param.15) | copy-start | bytes 110596
  2.9 21.8 %all-to-all-start = ((bf16[8,32,904]{2,1,0:T(8,128)(2,1)}), bf16[8,32,904]{2,1,0:T(8,128)(2,1)S(1)}, u32[]{:S(2)}, u32[]{:S(2)}) async-start(bf16[8,32,904]{2,1,0:T(8,128)(2,1)} %pad_maximum_fusion.2), calls=%async_computation | async-start | bytes 1048576 | tf_op jit(solution)/shard_map/all_to_all | solution.py:621
  10.3 8.7 %slice-start.8 = ((s8[7864320]{0:T(1024)(128)(4,1)}), s8[4194304]{0:T(1024)(128)(4,1)S(1)}, s32[]{:S(2)}) async-start(s8[7864320]{0:T(1024)(128)(4,1)} %bitcast.120), calls=%async_computation.9 | async-start | bytes 8388608
  11.2 7.8 %slice-start.9 = ((s8[7864320]{0:T(1024)(128)(4,1)}), s8[3670016]{0:T(1024)(128)(4,1)S(1)}, s32[]{:S(2)}) async-start(s8[7864320]{0:T(1024)(128)(4,1)} %bitcast.120), calls=%async_computation.10 | async-start | bytes 7340032
  24.7 1.9 collective-permute-start.1
  26.7 9.4 %collective-permute-start.6 = (bf16[64,4096]{1,0:T(8,128)(2,1)S(1)}, bf16[64,4096]{1,0:T(8,128)(2,1)S(1)}, u32[]{:S(2)}, u32[]{:S(2)}) collective-permute-start(bf16[64,4096]{1,0:T(8,128)(2,1)S(1)} %get-tuple-element.153.refs_7_), channel_id=1, source_target_pairs={{0,4},{5,1},{4,8},{9,5},{8,12},{13,9},{12,14},{15,13},{14,10},{11,... | collective-permute-start | bytes 1572872 | tf_op jit(solution)/shard_map/ppermute | solution.py:81
  28.3 13.3 %collective-permute-start.2 = (bf16[64,4096]{1,0:T(8,128)(2,1)S(1)}, bf16[64,4096]{1,0:T(8,128)(2,1)S(1)}, u32[]{:S(2)}, u32[]{:S(2)}) collective-permute-start(bf16[64,4096]{1,0:T(8,128)(2,1)S(1)} %get-tuple-element.154.refs_0_), channel_id=1, source_target_pairs={{0,4},{5,1},{4,8},{9,5},{8,12},{13,9},{12,14},{15,13},{14,10},{11,... | collective-permute-start | bytes 1572872 | tf_op jit(solution)/shard_map/ppermute | solution.py:81
  33.2 32.9 %slice-start = ((s8[7340032]{0:T(1024)(128)(4,1)}), s8[4194304]{0:T(1024)(128)(4,1)S(1)}, s32[]{:S(2)}) async-start(s8[7340032]{0:T(1024)(128)(4,1)} %bitcast.98), calls=%async_computation.1 | async-start | bytes 8388608
  33.2 32.9 %slice-start.1 = ((s8[7340032]{0:T(1024)(128)(4,1)}), s8[3145728]{0:T(1024)(128)(4,1)S(1)}, s32[]{:S(2)}) async-start(s8[7340032]{0:T(1024)(128)(4,1)} %bitcast.98), calls=%async_computation.2 | async-start | bytes 6291456
  36.1 11.1 %collective-permute-start.7 = (bf16[64,4096]{1,0:T(8,128)(2,1)S(1)}, bf16[64,4096]{1,0:T(8,128)(2,1)S(1)}, u32[]{:S(2)}, u32[]{:S(2)}) collective-permute-start(bf16[64,4096]{1,0:T(8,128)(2,1)S(1)} %collective-permute-done.6.refs_8_), channel_id=1, source_target_pairs={{0,4},{5,1},{4,8},{9,5},{8,12},{13,9},{12,14},{15,13},{14,10},{11,... | collective-permute-start | bytes 1572872 | tf_op jit(solution)/shard_map/ppermute | solution.py:81
  37.6 9.6 %collective-permute-start.8 = (bf16[64,4096]{1,0:T(8,128)(2,1)S(1)}, bf16[64,4096]{1,0:T(8,128)(2,1)S(1)}, u32[]{:S(2)}, u32[]{:S(2)}) collective-permute-start(bf16[64,4096]{1,0:T(8,128)(2,1)S(1)} %collective-permute-done.6.refs_8_), channel_id=1, source_target_pairs={{0,1},{1,0},{2,3},{3,2},{4,5},{5,4},{6,7},{7,6},{8,9},{9,8},{10,11... | collective-permute-start | bytes 1572872 | tf_op jit(solution)/shard_map/ppermute | solution.py:85
  41.6 11.2 %collective-permute-start.3 = (bf16[64,4096]{1,0:T(8,128)(2,1)S(1)}, bf16[64,4096]{1,0:T(8,128)(2,1)S(1)}, u32[]{:S(2)}, u32[]{:S(2)}) collective-permute-start(bf16[64,4096]{1,0:T(8,128)(2,1)S(1)} %collective-permute-done.2.refs_1_), channel_id=1, source_target_pairs={{0,4},{5,1},{4,8},{9,5},{8,12},{13,9},{12,14},{15,13},{14,10},{11,... | collective-permute-start | bytes 1572872 | tf_op jit(solution)/shard_map/ppermute | solution.py:81
  43.1 9.7 %collective-permute-start.4 = (bf16[64,4096]{1,0:T(8,128)(2,1)S(1)}, bf16[64,4096]{1,0:T(8,128)(2,1)S(1)}, u32[]{:S(2)}, u32[]{:S(2)}) collective-permute-start(bf16[64,4096]{1,0:T(8,128)(2,1)S(1)} %collective-permute-done.2.refs_1_), channel_id=1, source_target_pairs={{0,1},{1,0},{2,3},{3,2},{4,5},{5,4},{6,7},{7,6},{8,9},{9,8},{10,11... | collective-permute-start | bytes 1572872 | tf_op jit(solution)/shard_map/ppermute | solution.py:85
  47.2 11.2 %collective-permute-start.9 = (bf16[64,4096]{1,0:T(8,128)(2,1)S(1)}, bf16[64,4096]{1,0:T(8,128)(2,1)S(1)}, u32[]{:S(2)}, u32[]{:S(2)}) collective-permute-start(bf16[64,4096]{1,0:T(8,128)(2,1)S(1)} %collective-permute-done.7.refs_10_), channel_id=1, source_target_pairs={{0,4},{5,1},{4,8},{9,5},{8,12},{13,9},{12,14},{15,13},{14,10},{11,... | collective-permute-start | bytes 1572872 | tf_op jit(solution)/shard_map/ppermute | solution.py:81
  52.8 11.2 %collective-permute-start.5 = (bf16[64,4096]{1,0:T(8,128)(2,1)S(1)}, bf16[64,4096]{1,0:T(8,128)(2,1)S(1)}, u32[]{:S(2)}, u32[]{:S(2)}) collective-permute-start(bf16[64,4096]{1,0:T(8,128)(2,1)S(1)} %collective-permute-done.3.refs_3_), channel_id=1, source_target_pairs={{0,4},{5,1},{4,8},{9,5},{8,12},{13,9},{12,14},{15,13},{14,10},{11,... | collective-permute-start | bytes 1572872 | tf_op jit(solution)/shard_map/ppermute | solution.py:81
  54.4 11.5 %collective-permute-start.13 = (bf16[64,4096]{1,0:T(8,128)(2,1)S(1)}, bf16[64,4096]{1,0:T(8,128)(2,1)S(1)}, u32[]{:S(2)}, u32[]{:S(2)}) collective-permute-start(bf16[64,4096]{1,0:T(8,128)(2,1)S(1)} %collective-permute-done.7.refs_10_), channel_id=1, source_target_pairs={{0,1},{1,0},{2,3},{3,2},{4,5},{5,4},{6,7},{7,6},{8,9},{9,8},{10,11... | collective-permute-start | bytes 1572872 | tf_op jit(solution)/shard_map/ppermute | solution.py:85
  54.4 11.8 %collective-permute-start.11 = (bf16[64,4096]{1,0:T(8,128)(2,1)S(1)}, bf16[64,4096]{1,0:T(8,128)(2,1)S(1)}, u32[]{:S(2)}, u32[]{:S(2)}) collective-permute-start(bf16[64,4096]{1,0:T(8,128)(2,1)S(1)} %collective-permute-done.3.refs_3_), channel_id=1, source_target_pairs={{0,1},{1,0},{2,3},{3,2},{4,5},{5,4},{6,7},{7,6},{8,9},{9,8},{10,11... | collective-permute-start | bytes 1572872 | tf_op jit(solution)/shard_map/ppermute | solution.py:85
  58.4 7.7 %collective-permute-start.14 = (bf16[64,4096]{1,0:T(8,128)(2,1)S(1)}, bf16[64,4096]{1,0:T(8,128)(2,1)S(1)}, u32[]{:S(2)}, u32[]{:S(2)}) collective-permute-start(bf16[64,4096]{1,0:T(8,128)(2,1)S(1)} %collective-permute-done.9.refs_12_), channel_id=1, source_target_pairs={{0,1},{1,0},{2,3},{3,2},{4,5},{5,4},{6,7},{7,6},{8,9},{9,8},{10,11... | collective-permute-start | bytes 1572872 | tf_op jit(solution)/shard_map/ppermute | solution.py:85
  64.1 2.1 collective-permute-start.12
  64.1 9.5 %collective-permute-start.10 = (bf16[64,4096]{1,0:T(8,128)(2,1)S(1)}, bf16[64,4096]{1,0:T(8,128)(2,1)}, u32[]{:S(2)}, u32[]{:S(2)}) collective-permute-start(bf16[64,4096]{1,0:T(8,128)(2,1)S(1)} %broadcast_select_fusion.6), channel_id=1, source_target_pairs={{0,4},{5,1},{4,8},{9,5},{8,12},{13,9},{12,14},{15,13},{14,10},{11,... | collective-permute-start | bytes 1572872 | tf_op jit(solution)/shard_map/ppermute | solution.py:81
  65.9 8.8 %collective-permute-start = (bf16[8,32,904]{2,1,0:T(8,128)(2,1)S(1)}, bf16[8,32,904]{2,1,0:T(8,128)(2,1)}, u32[]{:S(2)}, u32[]{:S(2)}) collective-permute-start(bf16[8,32,904]{2,1,0:T(8,128)(2,1)S(1)} %all-to-all-done), channel_id=1, source_target_pairs={{0,1},{1,0},{2,3},{3,2},{4,5},{5,4},{6,7},{7,6},{8,9},{9,8},{10,11... | collective-permute-start | bytes 1388552 | tf_op jit(solution)/shard_map/ppermute | solution.py:85
  73.6 3.8 %collective-permute-start.15 = (bf16[64,4096]{1,0:T(8,128)(2,1)}, bf16[64,4096]{1,0:T(8,128)(2,1)S(1)}, u32[]{:S(2)}, u32[]{:S(2)}) collective-permute-start(bf16[64,4096]{1,0:T(8,128)(2,1)} %collective-permute-done.10), channel_id=1, source_target_pairs={{0,1},{1,0},{2,3},{3,2},{4,5},{5,4},{6,7},{7,6},{8,9},{9,8},{10,11... | collective-permute-start | bytes 1572872 | tf_op jit(solution)/shard_map/ppermute | solution.py:85
  73.8 18.2 %copy-start.3 = (s32[25]{0:T(128)}, s32[25]{0:T(128)S(1)}, u32[]{:S(2)}) copy-start(s32[25]{0:T(128)S(1)} %stack.133.meta) | copy-start | bytes 304
  75.8 13.0 %collective-permute-start.16 = (bf16[448,448]{1,0:T(8,128)(2,1)S(1)}, bf16[448,448]{1,0:T(8,128)(2,1)S(1)}, u32[]{:S(2)}, u32[]{:S(2)}) collective-permute-start(bf16[448,448]{1,0:T(8,128)(2,1)S(1)} %convert_element_type.250), channel_id=1, source_target_pairs={{0,16},{16,0},{1,17},{17,1},{2,18},{18,2},{3,19},{19,3},{4,20},{20... | collective-permute-start | bytes 1204232 | tf_op jit(solution)/shard_map/ppermute | solution.py:666
  87.7 4.3 %collective-permute-start.17 = (bf16[64,448]{1,0:T(8,128)(2,1)S(1)}, bf16[64,448]{1,0:T(8,128)(2,1)S(1)}, u32[]{:S(2)}, u32[]{:S(2)}) collective-permute-start(bf16[64,448]{1,0:T(8,128)(2,1)S(1)} %convert_element_type.251), channel_id=1, source_target_pairs={{0,16},{16,0},{1,17},{17,1},{2,18},{18,2},{3,19},{19,3},{4,20},{20... | collective-permute-start | bytes 172040 | tf_op jit(solution)/shard_map/ppermute | solution.py:666
  93.4 1.3 collective-permute-start.18
  93.5 2.0 collective-permute-start.19
  96.0 11.5 %collective-permute-start.25 = (bf16[272,896]{1,0:T(8,128)(2,1)S(1)}, bf16[272,896]{1,0:T(8,128)(2,1)S(1)}, u32[]{:S(2)}, u32[]{:S(2)}) collective-permute-start(bf16[272,896]{1,0:T(8,128)(2,1)S(1)} %fusion.20.refs_9_.refs_8_), channel_id=1, source_target_pairs={{0,4},{5,1},{4,8},{9,5},{8,12},{13,9},{12,14},{15,13},{14,10},{11,... | collective-permute-start | bytes 1462280 | tf_op jit(solution)/shard_map/ppermute | solution.py:81
  97.6 12.4 %collective-permute-start.20 = (bf16[272,896]{1,0:T(8,128)(2,1)S(1)}, bf16[272,896]{1,0:T(8,128)(2,1)S(1)}, u32[]{:S(2)}, u32[]{:S(2)}) collective-permute-start(bf16[272,896]{1,0:T(8,128)(2,1)S(1)} %pad_maximum_fusion.4.refs_4_.refs_0_), channel_id=1, source_target_pairs={{0,4},{5,1},{4,8},{9,5},{8,12},{13,9},{12,14},{15,13},{14,10},{11,... | collective-permute-start | bytes 1462280 | tf_op jit(solution)/shard_map/ppermute | solution.py:81
  107.5 17.1 %copy-start.11 = (bf16[272,896]{1,0:T(8,128)(2,1)}, bf16[272,896]{1,0:T(8,128)(2,1)S(1)}, u32[]{:S(2)}) copy-start(bf16[272,896]{1,0:T(8,128)(2,1)S(1)} %collective-permute-done.25.refs_10_.refs_9_) | copy-start | bytes 1462276
  107.5 8.8 %collective-permute-start.26 = (bf16[272,896]{1,0:T(8,128)(2,1)S(1)}, bf16[272,896]{1,0:T(8,128)(2,1)S(1)}, u32[]{:S(2)}, u32[]{:S(2)}) collective-permute-start(bf16[272,896]{1,0:T(8,128)(2,1)S(1)} %collective-permute-done.25.refs_10_.refs_9_), channel_id=1, source_target_pairs={{0,4},{5,1},{4,8},{9,5},{8,12},{13,9},{12,14},{15,13},{14,10},{11,... | collective-permute-start | bytes 1462280 | tf_op jit(solution)/shard_map/ppermute | solution.py:81
  109.0 7.3 %collective-permute-start.27 = (bf16[272,896]{1,0:T(8,128)(2,1)S(1)}, bf16[272,896]{1,0:T(8,128)(2,1)S(1)}, u32[]{:S(2)}, u32[]{:S(2)}) collective-permute-start(bf16[272,896]{1,0:T(8,128)(2,1)S(1)} %collective-permute-done.25.refs_10_.refs_9_), channel_id=1, source_target_pairs={{0,1},{1,0},{2,3},{3,2},{4,5},{5,4},{6,7},{7,6},{8,9},{9,8},{10,11... | collective-permute-start | bytes 1462280 | tf_op jit(solution)/shard_map/ppermute | solution.py:85
  110.0 14.6 %copy-start.12 = (bf16[272,896]{1,0:T(8,128)(2,1)}, bf16[272,896]{1,0:T(8,128)(2,1)S(1)}, u32[]{:S(2)}) copy-start(bf16[272,896]{1,0:T(8,128)(2,1)S(1)} %collective-permute-done.20.refs_5_.refs_1_) | copy-start | bytes 1462276
  110.0 11.5 %collective-permute-start.21 = (bf16[272,896]{1,0:T(8,128)(2,1)S(1)}, bf16[272,896]{1,0:T(8,128)(2,1)S(1)}, u32[]{:S(2)}, u32[]{:S(2)}) collective-permute-start(bf16[272,896]{1,0:T(8,128)(2,1)S(1)} %collective-permute-done.20.refs_5_.refs_1_), channel_id=1, source_target_pairs={{0,4},{5,1},{4,8},{9,5},{8,12},{13,9},{12,14},{15,13},{14,10},{11,... | collective-permute-start | bytes 1462280 | tf_op jit(solution)/shard_map/ppermute | solution.py:81
  111.6 9.9 %collective-permute-start.22 = (bf16[272,896]{1,0:T(8,128)(2,1)S(1)}, bf16[272,896]{1,0:T(8,128)(2,1)S(1)}, u32[]{:S(2)}, u32[]{:S(2)}) collective-permute-start(bf16[272,896]{1,0:T(8,128)(2,1)S(1)} %collective-permute-done.20.refs_5_.refs_1_), channel_id=1, source_target_pairs={{0,1},{1,0},{2,3},{3,2},{4,5},{5,4},{6,7},{7,6},{8,9},{9,8},{10,11... | collective-permute-start | bytes 1462280 | tf_op jit(solution)/shard_map/ppermute | solution.py:85
  116.3 8.3 %copy-start.13 = (bf16[272,896]{1,0:T(8,128)(2,1)}, bf16[272,896]{1,0:T(8,128)(2,1)S(1)}, u32[]{:S(2)}) copy-start(bf16[272,896]{1,0:T(8,128)(2,1)S(1)} %collective-permute-done.26.refs_12_.refs_11_) | copy-start | bytes 1462276
  116.3 8.3 %copy-start.14 = (bf16[272,896]{1,0:T(8,128)(2,1)}, bf16[272,896]{1,0:T(8,128)(2,1)S(1)}, u32[]{:S(2)}) copy-start(bf16[272,896]{1,0:T(8,128)(2,1)S(1)} %collective-permute-done.27.refs_11_.refs_10_) | copy-start | bytes 1462276
  116.3 8.3 %collective-permute-start.29 = (bf16[272,896]{1,0:T(8,128)(2,1)S(1)}, bf16[272,896]{1,0:T(8,128)(2,1)S(1)}, u32[]{:S(2)}, u32[]{:S(2)}) collective-permute-start(bf16[272,896]{1,0:T(8,128)(2,1)S(1)} %collective-permute-done.26.refs_12_.refs_11_), channel_id=1, source_target_pairs={{0,1},{1,0},{2,3},{3,2},{4,5},{5,4},{6,7},{7,6},{8,9},{9,8},{10,11... | collective-permute-start | bytes 1462280 | tf_op jit(solution)/shard_map/ppermute | solution.py:85
  121.5 3.1 %collective-permute-start.23 = (bf16[272,896]{1,0:T(8,128)(2,1)S(1)}, bf16[272,896]{1,0:T(8,128)(2,1)S(1)}, u32[]{:S(2)}, u32[]{:S(2)}) collective-permute-start(bf16[272,896]{1,0:T(8,128)(2,1)S(1)} %collective-permute-done.21.refs_7_.refs_3_), channel_id=1, source_target_pairs={{0,1},{1,0},{2,3},{3,2},{4,5},{5,4},{6,7},{7,6},{8,9},{9,8},{10,11... | collective-permute-start | bytes 1462280 | tf_op jit(solution)/shard_map/ppermute | solution.py:85
  121.6 15.1 %collective-permute-start.28 = (bf16[272,896]{1,0:T(8,128)(2,1)S(1)}, bf16[272,896]{1,0:T(8,128)(2,1)S(1)}, u32[]{:S(2)}, u32[]{:S(2)}) collective-permute-start(bf16[272,896]{1,0:T(8,128)(2,1)S(1)} %collective-permute-done.26.refs_12_.refs_11_), channel_id=1, source_target_pairs={{0,4},{5,1},{4,8},{9,5},{8,12},{13,9},{12,14},{15,13},{14,10},{11,... | collective-permute-start | bytes 1462280 | tf_op jit(solution)/shard_map/ppermute | solution.py:81
  123.1 13.6 %collective-permute-start.24 = (bf16[272,896]{1,0:T(8,128)(2,1)S(1)}, bf16[272,896]{1,0:T(8,128)(2,1)S(1)}, u32[]{:S(2)}, u32[]{:S(2)}) collective-permute-start(bf16[272,896]{1,0:T(8,128)(2,1)S(1)} %collective-permute-done.21.refs_7_.refs_3_), channel_id=1, source_target_pairs={{0,4},{5,1},{4,8},{9,5},{8,12},{13,9},{12,14},{15,13},{14,10},{11,... | collective-permute-start | bytes 1462280 | tf_op jit(solution)/shard_map/ppermute | solution.py:81
  136.7 13.5 %copy-start.6 = (bf16[272,896]{1,0:T(8,128)(2,1)}, bf16[272,896]{1,0:T(8,128)(2,1)S(1)}, u32[]{:S(2)}) copy-start(bf16[272,896]{1,0:T(8,128)(2,1)S(1)} %collective-permute-done.28.refs_7_.refs_13_) | copy-start | bytes 1462276
  136.8 13.4 %copy-start.7 = (bf16[272,896]{1,0:T(8,128)(2,1)}, bf16[272,896]{1,0:T(8,128)(2,1)S(1)}, u32[]{:S(2)}) copy-start(bf16[272,896]{1,0:T(8,128)(2,1)S(1)} %collective-permute-done.24.refs_4_.refs_5_) | copy-start | bytes 1462276
  136.8 9.1 %collective-permute-start.31 = (bf16[272,896]{1,0:T(8,128)(2,1)S(1)}, bf16[272,896]{1,0:T(8,128)(2,1)S(1)}, u32[]{:S(2)}, u32[]{:S(2)}) collective-permute-start(bf16[272,896]{1,0:T(8,128)(2,1)S(1)} %broadcast_select_fusion.9), channel_id=1, source_target_pairs={{0,4},{5,1},{4,8},{9,5},{8,12},{13,9},{12,14},{15,13},{14,10},{11,... | collective-permute-start | bytes 1462280 | tf_op jit(solution)/shard_map/ppermute | solution.py:81
  145.9 2.0 collective-permute-start.32
  145.9 3.2 %collective-permute-start.30 = (bf16[272,896]{1,0:T(8,128)(2,1)S(1)}, bf16[272,896]{1,0:T(8,128)(2,1)S(1)}, u32[]{:S(2)}, u32[]{:S(2)}) collective-permute-start(bf16[272,896]{1,0:T(8,128)(2,1)S(1)} %collective-permute-done.24.refs_4_.refs_5_), channel_id=1, source_target_pairs={{0,1},{1,0},{2,3},{3,2},{4,5},{5,4},{6,7},{7,6},{8,9},{9,8},{10,11... | collective-permute-start | bytes 1462280 | tf_op jit(solution)/shard_map/ppermute | solution.py:85
  146.7 3.6 %collective-permute-start.33 = (bf16[272,896]{1,0:T(8,128)(2,1)S(1)}, bf16[272,896]{1,0:T(8,128)(2,1)S(1)}, u32[]{:S(2)}, u32[]{:S(2)}) collective-permute-start(bf16[272,896]{1,0:T(8,128)(2,1)S(1)} %collective-permute-done.28.refs_7_.refs_13_), channel_id=1, source_target_pairs={{0,1},{1,0},{2,3},{3,2},{4,5},{5,4},{6,7},{7,6},{8,9},{9,8},{10,11... | collective-permute-start | bytes 1462280 | tf_op jit(solution)/shard_map/ppermute | solution.py:85
  166.8 13.5 %copy-start.21 = (bf16[96,7168]{1,0:T(8,128)(2,1)S(1)}, bf16[96,7168]{1,0:T(8,128)(2,1)}, u32[]{:S(2)}) copy-start(bf16[96,7168]{1,0:T(8,128)(2,1)} %get-tuple-element.116) | copy-start | bytes 4128772
  166.8 3.5 %collective-permute-start.35 = (bf16[96,7168]{1,0:T(8,128)(2,1)}, bf16[96,7168]{1,0:T(8,128)(2,1)}, u32[]{:S(2)}, u32[]{:S(2)}) collective-permute-start(bf16[96,7168]{1,0:T(8,128)(2,1)} %get-tuple-element.117), channel_id=1, source_target_pairs={{0,1},{1,0},{2,3},{3,2},{4,5},{5,4},{6,7},{7,6},{8,9},{9,8},{10,11... | collective-permute-start | bytes 4128776 | tf_op jit(solution)/shard_map/ppermute | solution.py:85
  171.7 6.1 %collective-permute-start.36 = (bf16[32,3584]{1,0:T(8,128)(2,1)S(1)}, bf16[32,3584]{1,0:T(8,128)(2,1)S(1)}, u32[]{:S(2)}, u32[]{:S(2)}) collective-permute-start(bf16[32,3584]{1,0:T(8,128)(2,1)S(1)} %get-tuple-element.148), channel_id=1, source_target_pairs={{0,4},{5,1},{4,8},{9,5},{8,12},{13,9},{12,14},{15,13},{14,10},{11,... | collective-permute-start | bytes 688136 | tf_op jit(solution)/shard_map/ppermute | solution.py:81
  173.9 6.4 %collective-permute-start.37 = (bf16[32,3584]{1,0:T(8,128)(2,1)S(1)}, bf16[32,3584]{1,0:T(8,128)(2,1)S(1)}, u32[]{:S(2)}, u32[]{:S(2)}) collective-permute-start(bf16[32,3584]{1,0:T(8,128)(2,1)S(1)} %get-tuple-element.147), channel_id=1, source_target_pairs={{0,4},{5,1},{4,8},{9,5},{8,12},{13,9},{12,14},{15,13},{14,10},{11,... | collective-permute-start | bytes 688136 | tf_op jit(solution)/shard_map/ppermute | solution.py:81
  174.4 15.7 %collective-permute-start.34 = (bf16[160,7168]{1,0:T(8,128)(2,1)}, bf16[160,7168]{1,0:T(8,128)(2,1)S(1)}, u32[]{:S(2)}, u32[]{:S(2)}) collective-permute-start(bf16[160,7168]{1,0:T(8,128)(2,1)} %get-tuple-element.115), channel_id=1, source_target_pairs={{0,1},{1,0},{2,3},{3,2},{4,5},{5,4},{6,7},{7,6},{8,9},{9,8},{10,11... | collective-permute-start | bytes 6881288 | tf_op jit(solution)/shard_map/ppermute | solution.py:85
  181.6 8.5 %collective-permute-start.39 = (bf16[64,3584]{1,0:T(8,128)(2,1)S(1)}, bf16[64,3584]{1,0:T(8,128)(2,1)S(1)}, u32[]{:S(2)}, u32[]{:S(2)}) collective-permute-start(bf16[64,3584]{1,0:T(8,128)(2,1)S(1)} %add_convert_fusion.6), channel_id=1, source_target_pairs={{0,4},{5,1},{4,8},{9,5},{8,12},{13,9},{12,14},{15,13},{14,10},{11,... | collective-permute-start | bytes 1376264 | tf_op jit(solution)/shard_map/ppermute | solution.py:81
  185.0 10.1 %collective-permute-start.38 = (bf16[64,3584]{1,0:T(8,128)(2,1)S(1)}, bf16[64,3584]{1,0:T(8,128)(2,1)S(1)}, u32[]{:S(2)}, u32[]{:S(2)}) collective-permute-start(bf16[64,3584]{1,0:T(8,128)(2,1)S(1)} %add_convert_fusion.5), channel_id=1, source_target_pairs={{0,4},{5,1},{4,8},{9,5},{8,12},{13,9},{12,14},{15,13},{14,10},{11,... | collective-permute-start | bytes 1376264 | tf_op jit(solution)/shard_map/ppermute | solution.py:81
  190.3 9.6 %collective-permute-start.41 = (bf16[64,3584]{1,0:T(8,128)(2,1)S(1)}, bf16[64,3584]{1,0:T(8,128)(2,1)S(1)}, u32[]{:S(2)}, u32[]{:S(2)}) collective-permute-start(bf16[64,3584]{1,0:T(8,128)(2,1)S(1)} %add_convert_fusion.4), channel_id=1, source_target_pairs={{0,4},{5,1},{4,8},{9,5},{8,12},{13,9},{12,14},{15,13},{14,10},{11,... | collective-permute-start | bytes 1376264 | tf_op jit(solution)/shard_map/ppermute | solution.py:81
  195.2 9.7 %collective-permute-start.40 = (bf16[64,3584]{1,0:T(8,128)(2,1)S(1)}, bf16[64,3584]{1,0:T(8,128)(2,1)S(1)}, u32[]{:S(2)}, u32[]{:S(2)}) collective-permute-start(bf16[64,3584]{1,0:T(8,128)(2,1)S(1)} %add_convert_fusion.3), channel_id=1, source_target_pairs={{0,4},{5,1},{4,8},{9,5},{8,12},{13,9},{12,14},{15,13},{14,10},{11,... | collective-permute-start | bytes 1376264 | tf_op jit(solution)/shard_map/ppermute | solution.py:81
  200.1 9.6 %collective-permute-start.42 = (bf16[64,3584]{1,0:T(8,128)(2,1)S(1)}, bf16[64,3584]{1,0:T(8,128)(2,1)S(1)}, u32[]{:S(2)}, u32[]{:S(2)}) collective-permute-start(bf16[64,3584]{1,0:T(8,128)(2,1)S(1)} %add_convert_fusion.2), channel_id=1, source_target_pairs={{0,4},{5,1},{4,8},{9,5},{8,12},{13,9},{12,14},{15,13},{14,10},{11,... | collective-permute-start | bytes 1376264 | tf_op jit(solution)/shard_map/ppermute | solution.py:81
  204.9 16.8 %copy-start.1 = (bf16[32,64,576]{2,1,0:T(8,128)(2,1)S(1)}, bf16[32,64,576]{2,1,0:T(8,128)(2,1)}, u32[]{:S(2)}) copy-start(bf16[32,64,576]{2,1,0:T(8,128)(2,1)} %param.13) | copy-start | bytes 7077892
  209.8 2.2 %collective-permute-start.43 = (bf16[32,3584]{1,0:T(8,128)(2,1)S(1)}, bf16[32,3584]{1,0:T(8,128)(2,1)S(1)}, u32[]{:S(2)}, u32[]{:S(2)}) collective-permute-start(bf16[32,3584]{1,0:T(8,128)(2,1)S(1)} %broadcast_select_fusion.11), channel_id=1, source_target_pairs={{0,1},{1,0},{2,3},{3,2},{4,5},{5,4},{6,7},{7,6},{8,9},{9,8},{10,11... | collective-permute-start | bytes 688136 | tf_op jit(solution)/shard_map/ppermute | solution.py:85
  209.9 8.5 %collective-permute-start.45 = (bf16[64,3584]{1,0:T(8,128)(2,1)S(1)}, bf16[64,3584]{1,0:T(8,128)(2,1)S(1)}, u32[]{:S(2)}, u32[]{:S(2)}) collective-permute-start(bf16[64,3584]{1,0:T(8,128)(2,1)S(1)} %add_convert_fusion.1), channel_id=1, source_target_pairs={{0,4},{5,1},{4,8},{9,5},{8,12},{13,9},{12,14},{15,13},{14,10},{11,... | collective-permute-start | bytes 1376264 | tf_op jit(solution)/shard_map/ppermute | solution.py:81
  212.2 7.0 %collective-permute-start.44 = (bf16[32,3584]{1,0:T(8,128)(2,1)S(1)}, bf16[32,3584]{1,0:T(8,128)(2,1)S(1)}, u32[]{:S(2)}, u32[]{:S(2)}) collective-permute-start(bf16[32,3584]{1,0:T(8,128)(2,1)S(1)} %add_convert_fusion.8), channel_id=1, source_target_pairs={{0,16},{16,0},{1,17},{17,1},{2,18},{18,2},{3,19},{19,3},{4,20},{20... | collective-permute-start | bytes 688136 | tf_op jit(solution)/shard_map/ppermute | solution.py:185
  219.3 1.6 collective-permute-start.46
  (20 other events, 54.0 us)

commit v2 on v1

--- a/solution.py
+++ b/solution.py
@@ -712,7 +712,7 @@
             for t in range(STREAMS):
                 moving = quarter(moving, pieces[t][0])
         if (s, i) == (STREAMS - 1, final - 1):
-            blocks = [piece[: chips - 3] for piece in pieces]
+            blocks = [piece[: chips - 4] for piece in pieces]
             blocks, _ = lax.optimization_barrier((blocks, moving))
             sums.append(gate(meta, 0, blocks, total, gate_up, chips))
         return moving
@@ -721,8 +721,8 @@
     stats = jnp.concatenate([unpacked(part) for part in pieces], axis=1)
     keep_first, give_first, keep_then, give_then = tail(
         meta,
-        chips - 3,
-        [piece[chips - 3 :] for piece in pieces],
+        chips - 4,
+        [piece[chips - 4 :] for piece in pieces],
         total,
         gate_up,
         sums[0],

time: 223 us -> 224 us (level)
  waiting for transfers between devices: 78.3 us -> 83.5 us
  starting transfers between devices: 48.9 us -> 46.3 us
    ppermute x22, waiting for transfers between devices: 64.2 us -> 69.2 us  [ring_step(): return lax.ppermute(block, ('chip', 'core'), pairs)]
    ppermute x22, starting transfers between devices: 36.5 us -> 33.4 us  [ring_step(): return lax.ppermute(block, ('chip', 'core'), pairs)]
    unnamed x68 -> x62, local copies, waits for them, and re-layouts: 13.6 us -> 12.1 us
  transfers between devices with their start and end apart: 48 -> 48, of which waited for: 28 -> 31; matrix products, arithmetic and copies ran while one was open for 17% -> 17% of each run, Pallas kernels for 12% -> 12%
where the time goes in v2:
time: 224 us; the launch traced here: 223 us
  waiting for transfers between devices  83.5 us (37%)
  starting transfers between devices  46.3 us (21%)
  Pallas kernels  43.5 us (19%)
  local copies, waits for them, and re-layouts  18.4 us (8%)
  other arithmetic  18.4 us (8%)
  matrix products  12 us (5%)
    ppermute x22, waiting for transfers between devices, ring_step(): return lax.ppermute(block, ('chip', 'core'), pairs)  69.2 us
    ppermute x22, starting transfers between devices, ring_step(): return lax.ppermute(block, ('chip', 'core'), pairs)  33.4 us
    pallas_call x1, Pallas kernels, tail(): pl.pallas_call(functools.partial(tail_kernel, len(gate_up), first, count,...  16.3 us
    pallas_call x2, Pallas kernels, project(): pl.pallas_call(kernel, out_shape=jax.ShapeDtypeStruct((total, columns), j...  14.1 us
    unnamed x62, local copies, waits for them, and re-layouts  12.1 us
    ppermute x22, waiting for transfers between devices, swap_cores(): return lax.ppermute(block, 'core', SWAP)  9.3 us
    pallas_call x1, Pallas kernels, gate(): pl.pallas_call(functools.partial(gate_kernel, len(gate_up), first, count,...  9.27 us
    all_to_all x1, starting transfers between devices, body(): lax.all_to_all(jnp.concatenate([outgoing, names], axis=2), 'chip', split_...  7.29 us
  transfers between devices with their start and end apart: 48, of which 31 were waited for; matrix products, arithmetic and copies ran while one was open for 17% of the time, Pallas kernels for 12%

profile of v2, /device:TPU:0, one launch (start us, length us, event | category | flops | bytes accessed | tf_op | source)
XLA Modules:
  0.0 222.8 jit_solution(2759377712473624334)
XLA Ops:
  0.0 1.2 copy.56
  2.9 7.3 %all-to-all-start = ((bf16[8,32,904]{2,1,0:T(8,128)(2,1)}), bf16[8,32,904]{2,1,0:T(8,128)(2,1)S(1)}, u32[]{:S(2)}, u32[]{:S(2)}) async-start(bf16[8,32,904]{2,1,0:T(8,128)(2,1)} %pad_maximum_fusion.2), calls=%async_computation | async-start | bytes 1048576 | tf_op jit(solution)/shard_map/all_to_all | solution.py:621
  11.2 6.8 %fusion.6 = (f32[32,64]{1,0:T(8,128)S(1)}, f32[32,64,192]{2,1,0:T(8,128)S(1)}) fusion(pred[32,192]{1,0:T(8,128)(4,1)S(1)} %iota_compare_fusion.1, bf16[32,64,576]{2,1,0:T(8,128)(2,1)S(1)} %copy-done, bf16[32,192,576]{2,1,0:T(8,128)(2,1)} %param.14), kind=kOutput, calls=%fused_computation.8 | convolution fusion | flops 454162432 | bytes 11024384 | tf_op jit(solution)/shard_map/thk,tjk->thj/dot_general | solution.py:33
  19.0 2.0 add_convert_fusion
  21.7 2.3 %fusion.11 = bf16[64,4,8,128]{3,2,1,0:T(8,128)(2,1)S(1)} fusion(bf16[64,512,128]{2,1,0:T(8,128)(2,1)S(1)} %bitcast.115, bf16[32,64,512]{2,1,0:T(8,128)(2,1)S(1)} %add_convert_fusion), kind=kOutput, calls=%fused_computation.11 | convolution fusion | flops 268697600 | bytes 11010048 | tf_op jit(solution)/shard_map/thc,hcd->thd/dot_general | solution.py:59
  24.7 1.9 collective-permute-done.1
  26.7 1.6 collective-permute-start.6
  28.3 1.5 collective-permute-start.2
  30.4 2.8 %copy.41 = bf16[224,8,2,512]{3,1,2,0:T(8,128)(2,1)} copy(bf16[224,8,2,512]{3,2,1,0:T(2,128)(2,1)S(1)} %bitcast.116) | data formatting | bytes 7340032
  33.2 2.9 %copy.42 = bf16[224,8,2,512]{3,1,2,0:T(8,128)(2,1)} copy(bf16[224,8,2,512]{3,2,1,0:T(2,128)(2,1)S(1)} %bitcast.117) | data formatting | bytes 7340032
  36.1 1.5 collective-permute-start.7
  37.6 4.0 %collective-permute-done.2.refs_1_ = bf16[64,4096]{1,0:T(8,128)(2,1)S(1)} collective-permute-done((bf16[64,4096]{1,0:T(8,128)(2,1)S(1)}, bf16[64,4096]{1,0:T(8,128)(2,1)S(1)}, u32[]{:S(2)}, u32[]{:S(2)}) %collective-permute-start.2) | collective-permute-done | bytes 524320 | tf_op jit(solution)/shard_map/ppermute | solution.py:81
  41.6 1.5 collective-permute-start.3
  43.1 4.1 %collective-permute-done.7.refs_10_ = bf16[64,4096]{1,0:T(8,128)(2,1)S(1)} collective-permute-done((bf16[64,4096]{1,0:T(8,128)(2,1)S(1)}, bf16[64,4096]{1,0:T(8,128)(2,1)S(1)}, u32[]{:S(2)}, u32[]{:S(2)}) %collective-permute-start.7) | collective-permute-done | bytes 524320 | tf_op jit(solution)/shard_map/ppermute | solution.py:81
  47.2 1.5 collective-permute-start.9
  48.8 4.1 %collective-permute-done.3.refs_3_ = bf16[64,4096]{1,0:T(8,128)(2,1)S(1)} collective-permute-done((bf16[64,4096]{1,0:T(8,128)(2,1)S(1)}, bf16[64,4096]{1,0:T(8,128)(2,1)S(1)}, u32[]{:S(2)}, u32[]{:S(2)}) %collective-permute-start.3) | collective-permute-done | bytes 524320 | tf_op jit(solution)/shard_map/ppermute | solution.py:81
  52.8 1.5 collective-permute-start.5
  54.9 3.6 %collective-permute-done.9.refs_12_ = bf16[64,4096]{1,0:T(8,128)(2,1)S(1)} collective-permute-done((bf16[64,4096]{1,0:T(8,128)(2,1)S(1)}, bf16[64,4096]{1,0:T(8,128)(2,1)S(1)}, u32[]{:S(2)}, u32[]{:S(2)}) %collective-permute-start.9) | collective-permute-done | bytes 524320 | tf_op jit(solution)/shard_map/ppermute | solution.py:81
  58.5 5.6 %collective-permute-done.5.refs_5_ = bf16[64,4096]{1,0:T(8,128)(2,1)S(1)} collective-permute-done((bf16[64,4096]{1,0:T(8,128)(2,1)S(1)}, bf16[64,4096]{1,0:T(8,128)(2,1)S(1)}, u32[]{:S(2)}, u32[]{:S(2)}) %collective-permute-start.5) | collective-permute-done | bytes 524320 | tf_op jit(solution)/shard_map/ppermute | solution.py:81
  64.1 1.8 collective-permute-start.10
  66.2 6.9 %shard_map.118.refs_0_ = f32[448,448]{1,0:T(8,128)S(1)} custom-call(bf16[448,8192]{1,0:T(8,128)(2,1)S(1)} %bitcast.100, bf16[64,4096]{1,0:T(8,128)(2,1)S(1)} %get-tuple-element.150.refs_0_, bf16[64,4096]{1,0:T(8,128)(2,1)S(1)} %collective-permute-done.2.refs_1_, bf16[64,4096]{1,0:T(8,128)(2,1)S(1)} %collective-permute-done.4.refs_2_, ...), custom_call_target="tpu_custom_call" | custom-call | flops 3288334336 | bytes 15482880 | tf_op jit(solution)/shard_map/pallas_call | solution.py:285
  75.9 1.6 collective-permute-start.16
  77.4 2.1 broadcast_select_fusion.4
  79.5 7.3 %shard_map.119.refs_1_ = f32[64,448]{1,0:T(8,128)} custom-call(bf16[448,8192]{1,0:T(8,128)(2,1)} %bitcast.97, bf16[64,4096]{1,0:T(8,128)(2,1)} %get-tuple-element.148.refs_0_, bf16[64,4096]{1,0:T(8,128)(2,1)} %get-tuple-element.147.refs_1_), custom_call_target="tpu_custom_call" | custom-call | flops 469762048 | bytes 8503296 | tf_op jit(solution)/shard_map/pallas_call | solution.py:285
  88.9 3.2 %collective-permute-done.17.refs_3_ = bf16[64,448]{1,0:T(8,128)(2,1)S(1)} collective-permute-done((bf16[64,448]{1,0:T(8,128)(2,1)S(1)}, bf16[64,448]{1,0:T(8,128)(2,1)S(1)}, u32[]{:S(2)}, u32[]{:S(2)}) %collective-permute-start.17) | collective-permute-done | bytes 57376 | tf_op jit(solution)/shard_map/ppermute | solution.py:666
  92.1 1.3 shard_map.120
  96.0 1.6 collective-permute-start.25
  97.6 1.5 collective-permute-start.20
  99.8 2.8 %copy.43 = bf16[224,8,2,512]{3,1,2,0:T(8,128)(2,1)} copy(bf16[224,8,2,512]{3,2,1,0:T(2,128)(2,1)S(1)} %bitcast.118) | data formatting | bytes 7340032
  102.7 2.0 slice-done.7
  104.7 2.8 %copy.44 = bf16[224,8,2,512]{3,1,2,0:T(8,128)(2,1)} copy(bf16[224,8,2,512]{3,2,1,0:T(2,128)(2,1)S(1)} %bitcast.119) | data formatting | bytes 7340032
  107.5 1.5 collective-permute-start.26
  110.1 1.5 collective-permute-start.21
  111.6 4.8 %collective-permute-done.26.refs_11_ = bf16[272,896]{1,0:T(8,128)(2,1)} collective-permute-done((bf16[272,896]{1,0:T(8,128)(2,1)S(1)}, bf16[272,896]{1,0:T(8,128)(2,1)}, u32[]{:S(2)}, u32[]{:S(2)}) %collective-permute-start.26) | collective-permute-done | bytes 487456 | tf_op jit(solution)/shard_map/ppermute | solution.py:81
  116.4 5.1 %collective-permute-done.21.refs_7_.refs_3_ = bf16[272,896]{1,0:T(8,128)(2,1)S(1)} collective-permute-done((bf16[272,896]{1,0:T(8,128)(2,1)S(1)}, bf16[272,896]{1,0:T(8,128)(2,1)S(1)}, u32[]{:S(2)}, u32[]{:S(2)}) %collective-permute-start.21) | collective-permute-done | bytes 487456 | tf_op jit(solution)/shard_map/ppermute | solution.py:81
  121.6 1.5 collective-permute-start.28
  123.1 1.5 collective-permute-start.24
  124.6 9.3 %shard_map.121.before = f32[512,1024]{1,0:T(8,128)} custom-call(s32[25]{0:T(128)} %copy-done.3, bf16[1792,1024]{1,0:T(8,128)(2,1)} %bitcast.106, bf16[1792,1024]{1,0:T(8,128)(2,1)} %bitcast.108, bf16[1792,1024]{1,0:T(8,128)(2,1)} %bitcast.110, bf16[1792,1024]{1,0:T(8,128)(2,1)} %bitcast.112, bf16[272,896]{1,0:T(8,128)(2,1)} %copy-done.9, ...), custom_call_target="tpu_custom_call" | custom-call | flops 3758096384 | bytes 11010048 | tf_op jit(solution)/shard_map/pallas_call | solution.py:451
  133.9 1.9 collective-permute-done.24.refs_5_
  135.9 1.5 collective-permute-start.30
  137.4 7.3 %collective-permute-done.30 = bf16[272,896]{1,0:T(8,128)(2,1)S(1)} collective-permute-done((bf16[272,896]{1,0:T(8,128)(2,1)S(1)}, bf16[272,896]{1,0:T(8,128)(2,1)S(1)}, u32[]{:S(2)}, u32[]{:S(2)}) %collective-permute-start.30) | collective-permute-done | bytes 487456 | tf_op jit(solution)/shard_map/ppermute | solution.py:81
  146.7 1.3 broadcast_select_fusion.8
  151.4 16.3 %shard_map.122 = (bf16[96,7168]{1,0:T(8,128)(2,1)}, bf16[96,7168]{1,0:T(8,128)(2,1)}, bf16[160,7168]{1,0:T(8,128)(2,1)}, bf16[160,7168]{1,0:T(8,128)(2,1)}) custom-call(s32[25]{0:T(128)} %copy-done.3, f32[2,512]{1,0:T(2,128)} %pad_maximum_fusion.9.factors, f32[512,1024]{1,0:T(8,128)} %shard_map.121.before, bf16[512,7168]{1,0:T(8,128)(2,1)} %bitcast.122, ...), custom_call_target="tpu_custom_call" | custom-call | flops 7516192768 | bytes 25690112 | tf_op jit(solution)/shard_map/pallas_call | solution.py:559
  167.9 3.3 %collective-permute-done.35 = bf16[96,7168]{1,0:T(8,128)(2,1)} collective-permute-done((bf16[96,7168]{1,0:T(8,128)(2,1)}, bf16[96,7168]{1,0:T(8,128)(2,1)}, u32[]{:S(2)}, u32[]{:S(2)}) %collective-permute-start.35) | collective-permute-done | bytes 1376288 | tf_op jit(solution)/shard_map/ppermute | solution.py:85
  171.2 1.4 add_convert_fusion.9
  172.6 1.7 collective-permute-start.36
  174.3 1.5 collective-permute-start.37
  175.8 3.1 %collective-permute-done.36 = bf16[32,3584]{1,0:T(8,128)(2,1)S(1)} collective-permute-done((bf16[32,3584]{1,0:T(8,128)(2,1)S(1)}, bf16[32,3584]{1,0:T(8,128)(2,1)S(1)}, u32[]{:S(2)}, u32[]{:S(2)}) %collective-permute-start.36) | collective-permute-done | bytes 229408 | tf_op jit(solution)/shard_map/ppermute | solution.py:81
  178.9 2.5 %collective-permute-done.37 = bf16[32,3584]{1,0:T(8,128)(2,1)S(1)} collective-permute-done((bf16[32,3584]{1,0:T(8,128)(2,1)S(1)}, bf16[32,3584]{1,0:T(8,128)(2,1)S(1)}, u32[]{:S(2)}, u32[]{:S(2)}) %collective-permute-start.37) | collective-permute-done | bytes 229408 | tf_op jit(solution)/shard_map/ppermute | solution.py:81
  181.5 1.2 add_convert_fusion.6
  182.7 1.4 collective-permute-start.39
  184.2 1.2 add_convert_fusion.5
  185.4 1.5 collective-permute-start.38
  186.9 2.5 %shard_map.123 = bf16[8,32,896]{2,1,0:T(8,128)(2,1)} custom-call(s32[25]{0:T(128)} %copy-done.3, bf16[272,896]{1,0:T(8,128)(2,1)} %copy-done.9, bf16[272,896]{1,0:T(8,128)(2,1)} %copy-done.12, bf16[272,896]{1,0:T(8,128)(2,1)} %copy-done.15, bf16[272,896]{1,0:T(8,128)(2,1)} %copy-done.14, bf16[272,896]{1,0:T(8,128)(2,1)} %copy-done.16, ...), custom_call_target="tpu_custom_call" | custom-call | tf_op jit(solution)/shard_map/pallas_call | solution.py:367
  191.4 1.4 collective-permute-start.41
  192.9 3.3 %collective-permute-done.38 = bf16[64,3584]{1,0:T(8,128)(2,1)S(1)} collective-permute-done((bf16[64,3584]{1,0:T(8,128)(2,1)S(1)}, bf16[64,3584]{1,0:T(8,128)(2,1)S(1)}, u32[]{:S(2)}, u32[]{:S(2)}) %collective-permute-start.38) | collective-permute-done | bytes 458784 | tf_op jit(solution)/shard_map/ppermute | solution.py:81
  196.3 1.4 collective-permute-start.40
  197.8 3.3 %collective-permute-done.41 = bf16[64,3584]{1,0:T(8,128)(2,1)S(1)} collective-permute-done((bf16[64,3584]{1,0:T(8,128)(2,1)S(1)}, bf16[64,3584]{1,0:T(8,128)(2,1)S(1)}, u32[]{:S(2)}, u32[]{:S(2)}) %collective-permute-start.41) | collective-permute-done | bytes 458784 | tf_op jit(solution)/shard_map/ppermute | solution.py:81
  201.2 1.4 collective-permute-start.42
  202.7 3.3 %collective-permute-done.40 = bf16[64,3584]{1,0:T(8,128)(2,1)S(1)} collective-permute-done((bf16[64,3584]{1,0:T(8,128)(2,1)S(1)}, bf16[64,3584]{1,0:T(8,128)(2,1)S(1)}, u32[]{:S(2)}, u32[]{:S(2)}) %collective-permute-start.40) | collective-permute-done | bytes 458784 | tf_op jit(solution)/shard_map/ppermute | solution.py:81
  206.1 4.7 %collective-permute-done.42 = bf16[64,3584]{1,0:T(8,128)(2,1)S(1)} collective-permute-done((bf16[64,3584]{1,0:T(8,128)(2,1)S(1)}, bf16[64,3584]{1,0:T(8,128)(2,1)S(1)}, u32[]{:S(2)}, u32[]{:S(2)}) %collective-permute-start.42) | collective-permute-done | bytes 458784 | tf_op jit(solution)/shard_map/ppermute | solution.py:81
  211.0 1.4 collective-permute-start.45
  213.2 6.3 %collective-permute-done.45 = bf16[64,3584]{1,0:T(8,128)(2,1)S(1)} collective-permute-done((bf16[64,3584]{1,0:T(8,128)(2,1)S(1)}, bf16[64,3584]{1,0:T(8,128)(2,1)S(1)}, u32[]{:S(2)}, u32[]{:S(2)}) %collective-permute-start.45) | collective-permute-done | bytes 458784 | tf_op jit(solution)/shard_map/ppermute | solution.py:81
  220.5 1.5 collective-permute-done.46
  (190 shorter events, 26.6 us)
Async XLA Ops:
  0.0 10.3 %copy-start = (bf16[32,64,576]{2,1,0:T(8,128)(2,1)S(1)}, bf16[32,64,576]{2,1,0:T(8,128)(2,1)}, u32[]{:S(2)}) copy-start(bf16[32,64,576]{2,1,0:T(8,128)(2,1)} %param.13) | copy-start | bytes 7077892
  0.0 10.2 %copy-start.22 = (s32[32]{0:T(128)S(1)}, s32[32]{0:T(128)}, u32[]{:S(2)}) copy-start(s32[32]{0:T(128)} %param.16) | copy-start | bytes 388
  0.0 10.3 %copy-start.20 = (bf16[32,576]{1,0:T(8,128)(2,1)S(1)}, bf16[32,576]{1,0:T(8,128)(2,1)}, u32[]{:S(2)}) copy-start(bf16[32,576]{1,0:T(8,128)(2,1)} %param.15) | copy-start | bytes 110596
  2.9 21.8 %all-to-all-start = ((bf16[8,32,904]{2,1,0:T(8,128)(2,1)}), bf16[8,32,904]{2,1,0:T(8,128)(2,1)S(1)}, u32[]{:S(2)}, u32[]{:S(2)}) async-start(bf16[8,32,904]{2,1,0:T(8,128)(2,1)} %pad_maximum_fusion.2), calls=%async_computation | async-start | bytes 1048576 | tf_op jit(solution)/shard_map/all_to_all | solution.py:621
  10.3 8.7 %slice-start.8 = ((s8[7864320]{0:T(1024)(128)(4,1)}), s8[4194304]{0:T(1024)(128)(4,1)S(1)}, s32[]{:S(2)}) async-start(s8[7864320]{0:T(1024)(128)(4,1)} %bitcast.120), calls=%async_computation.9 | async-start | bytes 8388608
  11.2 7.8 %slice-start.9 = ((s8[7864320]{0:T(1024)(128)(4,1)}), s8[3670016]{0:T(1024)(128)(4,1)S(1)}, s32[]{:S(2)}) async-start(s8[7864320]{0:T(1024)(128)(4,1)} %bitcast.120), calls=%async_computation.10 | async-start | bytes 7340032
  24.7 1.9 collective-permute-start.1
  26.7 9.4 %collective-permute-start.6 = (bf16[64,4096]{1,0:T(8,128)(2,1)S(1)}, bf16[64,4096]{1,0:T(8,128)(2,1)S(1)}, u32[]{:S(2)}, u32[]{:S(2)}) collective-permute-start(bf16[64,4096]{1,0:T(8,128)(2,1)S(1)} %get-tuple-element.149.refs_7_), channel_id=1, source_target_pairs={{0,4},{5,1},{4,8},{9,5},{8,12},{13,9},{12,14},{15,13},{14,10},{11,... | collective-permute-start | bytes 1572872 | tf_op jit(solution)/shard_map/ppermute | solution.py:81
  28.3 13.3 %collective-permute-start.2 = (bf16[64,4096]{1,0:T(8,128)(2,1)S(1)}, bf16[64,4096]{1,0:T(8,128)(2,1)S(1)}, u32[]{:S(2)}, u32[]{:S(2)}) collective-permute-start(bf16[64,4096]{1,0:T(8,128)(2,1)S(1)} %get-tuple-element.150.refs_0_), channel_id=1, source_target_pairs={{0,4},{5,1},{4,8},{9,5},{8,12},{13,9},{12,14},{15,13},{14,10},{11,... | collective-permute-start | bytes 1572872 | tf_op jit(solution)/shard_map/ppermute | solution.py:81
  33.2 32.9 %slice-start = ((s8[7340032]{0:T(1024)(128)(4,1)}), s8[4194304]{0:T(1024)(128)(4,1)S(1)}, s32[]{:S(2)}) async-start(s8[7340032]{0:T(1024)(128)(4,1)} %bitcast.98), calls=%async_computation.1 | async-start | bytes 8388608
  33.2 32.9 %slice-start.1 = ((s8[7340032]{0:T(1024)(128)(4,1)}), s8[3145728]{0:T(1024)(128)(4,1)S(1)}, s32[]{:S(2)}) async-start(s8[7340032]{0:T(1024)(128)(4,1)} %bitcast.98), calls=%async_computation.2 | async-start | bytes 6291456
  36.1 11.1 %collective-permute-start.7 = (bf16[64,4096]{1,0:T(8,128)(2,1)S(1)}, bf16[64,4096]{1,0:T(8,128)(2,1)S(1)}, u32[]{:S(2)}, u32[]{:S(2)}) collective-permute-start(bf16[64,4096]{1,0:T(8,128)(2,1)S(1)} %collective-permute-done.6.refs_8_), channel_id=1, source_target_pairs={{0,4},{5,1},{4,8},{9,5},{8,12},{13,9},{12,14},{15,13},{14,10},{11,... | collective-permute-start | bytes 1572872 | tf_op jit(solution)/shard_map/ppermute | solution.py:81
  37.6 9.6 %collective-permute-start.8 = (bf16[64,4096]{1,0:T(8,128)(2,1)S(1)}, bf16[64,4096]{1,0:T(8,128)(2,1)S(1)}, u32[]{:S(2)}, u32[]{:S(2)}) collective-permute-start(bf16[64,4096]{1,0:T(8,128)(2,1)S(1)} %collective-permute-done.6.refs_8_), channel_id=1, source_target_pairs={{0,1},{1,0},{2,3},{3,2},{4,5},{5,4},{6,7},{7,6},{8,9},{9,8},{10,11... | collective-permute-start | bytes 1572872 | tf_op jit(solution)/shard_map/ppermute | solution.py:85
  41.6 11.2 %collective-permute-start.3 = (bf16[64,4096]{1,0:T(8,128)(2,1)S(1)}, bf16[64,4096]{1,0:T(8,128)(2,1)S(1)}, u32[]{:S(2)}, u32[]{:S(2)}) collective-permute-start(bf16[64,4096]{1,0:T(8,128)(2,1)S(1)} %collective-permute-done.2.refs_1_), channel_id=1, source_target_pairs={{0,4},{5,1},{4,8},{9,5},{8,12},{13,9},{12,14},{15,13},{14,10},{11,... | collective-permute-start | bytes 1572872 | tf_op jit(solution)/shard_map/ppermute | solution.py:81
  43.1 9.7 %collective-permute-start.4 = (bf16[64,4096]{1,0:T(8,128)(2,1)S(1)}, bf16[64,4096]{1,0:T(8,128)(2,1)S(1)}, u32[]{:S(2)}, u32[]{:S(2)}) collective-permute-start(bf16[64,4096]{1,0:T(8,128)(2,1)S(1)} %collective-permute-done.2.refs_1_), channel_id=1, source_target_pairs={{0,1},{1,0},{2,3},{3,2},{4,5},{5,4},{6,7},{7,6},{8,9},{9,8},{10,11... | collective-permute-start | bytes 1572872 | tf_op jit(solution)/shard_map/ppermute | solution.py:85
  47.2 11.2 %collective-permute-start.9 = (bf16[64,4096]{1,0:T(8,128)(2,1)S(1)}, bf16[64,4096]{1,0:T(8,128)(2,1)S(1)}, u32[]{:S(2)}, u32[]{:S(2)}) collective-permute-start(bf16[64,4096]{1,0:T(8,128)(2,1)S(1)} %collective-permute-done.7.refs_10_), channel_id=1, source_target_pairs={{0,4},{5,1},{4,8},{9,5},{8,12},{13,9},{12,14},{15,13},{14,10},{11,... | collective-permute-start | bytes 1572872 | tf_op jit(solution)/shard_map/ppermute | solution.py:81
  52.8 11.2 %collective-permute-start.5 = (bf16[64,4096]{1,0:T(8,128)(2,1)S(1)}, bf16[64,4096]{1,0:T(8,128)(2,1)S(1)}, u32[]{:S(2)}, u32[]{:S(2)}) collective-permute-start(bf16[64,4096]{1,0:T(8,128)(2,1)S(1)} %collective-permute-done.3.refs_3_), channel_id=1, source_target_pairs={{0,4},{5,1},{4,8},{9,5},{8,12},{13,9},{12,14},{15,13},{14,10},{11,... | collective-permute-start | bytes 1572872 | tf_op jit(solution)/shard_map/ppermute | solution.py:81
  54.4 11.5 %collective-permute-start.13 = (bf16[64,4096]{1,0:T(8,128)(2,1)S(1)}, bf16[64,4096]{1,0:T(8,128)(2,1)S(1)}, u32[]{:S(2)}, u32[]{:S(2)}) collective-permute-start(bf16[64,4096]{1,0:T(8,128)(2,1)S(1)} %collective-permute-done.7.refs_10_), channel_id=1, source_target_pairs={{0,1},{1,0},{2,3},{3,2},{4,5},{5,4},{6,7},{7,6},{8,9},{9,8},{10,11... | collective-permute-start | bytes 1572872 | tf_op jit(solution)/shard_map/ppermute | solution.py:85
  54.4 11.8 %collective-permute-start.11 = (bf16[64,4096]{1,0:T(8,128)(2,1)S(1)}, bf16[64,4096]{1,0:T(8,128)(2,1)S(1)}, u32[]{:S(2)}, u32[]{:S(2)}) collective-permute-start(bf16[64,4096]{1,0:T(8,128)(2,1)S(1)} %collective-permute-done.3.refs_3_), channel_id=1, source_target_pairs={{0,1},{1,0},{2,3},{3,2},{4,5},{5,4},{6,7},{7,6},{8,9},{9,8},{10,11... | collective-permute-start | bytes 1572872 | tf_op jit(solution)/shard_map/ppermute | solution.py:85
  58.5 7.7 %collective-permute-start.14 = (bf16[64,4096]{1,0:T(8,128)(2,1)S(1)}, bf16[64,4096]{1,0:T(8,128)(2,1)S(1)}, u32[]{:S(2)}, u32[]{:S(2)}) collective-permute-start(bf16[64,4096]{1,0:T(8,128)(2,1)S(1)} %collective-permute-done.9.refs_12_), channel_id=1, source_target_pairs={{0,1},{1,0},{2,3},{3,2},{4,5},{5,4},{6,7},{7,6},{8,9},{9,8},{10,11... | collective-permute-start | bytes 1572872 | tf_op jit(solution)/shard_map/ppermute | solution.py:85
  64.1 2.1 collective-permute-start.12
  64.1 9.5 %collective-permute-start.10 = (bf16[64,4096]{1,0:T(8,128)(2,1)S(1)}, bf16[64,4096]{1,0:T(8,128)(2,1)}, u32[]{:S(2)}, u32[]{:S(2)}) collective-permute-start(bf16[64,4096]{1,0:T(8,128)(2,1)S(1)} %broadcast_select_fusion.6), channel_id=1, source_target_pairs={{0,4},{5,1},{4,8},{9,5},{8,12},{13,9},{12,14},{15,13},{14,10},{11,... | collective-permute-start | bytes 1572872 | tf_op jit(solution)/shard_map/ppermute | solution.py:81
  65.9 8.8 %collective-permute-start = (bf16[8,32,904]{2,1,0:T(8,128)(2,1)S(1)}, bf16[8,32,904]{2,1,0:T(8,128)(2,1)}, u32[]{:S(2)}, u32[]{:S(2)}) collective-permute-start(bf16[8,32,904]{2,1,0:T(8,128)(2,1)S(1)} %all-to-all-done), channel_id=1, source_target_pairs={{0,1},{1,0},{2,3},{3,2},{4,5},{5,4},{6,7},{7,6},{8,9},{9,8},{10,11... | collective-permute-start | bytes 1388552 | tf_op jit(solution)/shard_map/ppermute | solution.py:85
  66.2 7.5 %copy-start.21 = (f32[7168]{0:T(1024)S(1)}, f32[7168]{0:T(1024)}, u32[]{:S(2)}) copy-start(f32[7168]{0:T(1024)} %param.19) | copy-start | bytes 86020
  73.7 3.8 %collective-permute-start.15 = (bf16[64,4096]{1,0:T(8,128)(2,1)}, bf16[64,4096]{1,0:T(8,128)(2,1)S(1)}, u32[]{:S(2)}, u32[]{:S(2)}) collective-permute-start(bf16[64,4096]{1,0:T(8,128)(2,1)} %collective-permute-done.10), channel_id=1, source_target_pairs={{0,1},{1,0},{2,3},{3,2},{4,5},{5,4},{6,7},{7,6},{8,9},{9,8},{10,11... | collective-permute-start | bytes 1572872 | tf_op jit(solution)/shard_map/ppermute | solution.py:85
  73.8 18.2 %copy-start.3 = (s32[25]{0:T(128)}, s32[25]{0:T(128)S(1)}, u32[]{:S(2)}) copy-start(s32[25]{0:T(128)S(1)} %stack.133.meta) | copy-start | bytes 304
  75.9 13.0 %collective-permute-start.16 = (bf16[448,448]{1,0:T(8,128)(2,1)S(1)}, bf16[448,448]{1,0:T(8,128)(2,1)S(1)}, u32[]{:S(2)}, u32[]{:S(2)}) collective-permute-start(bf16[448,448]{1,0:T(8,128)(2,1)S(1)} %convert_element_type.250), channel_id=1, source_target_pairs={{0,16},{16,0},{1,17},{17,1},{2,18},{18,2},{3,19},{19,3},{4,20},{20... | collective-permute-start | bytes 1204232 | tf_op jit(solution)/shard_map/ppermute | solution.py:666
  87.8 4.3 %collective-permute-start.17 = (bf16[64,448]{1,0:T(8,128)(2,1)S(1)}, bf16[64,448]{1,0:T(8,128)(2,1)S(1)}, u32[]{:S(2)}, u32[]{:S(2)}) collective-permute-start(bf16[64,448]{1,0:T(8,128)(2,1)S(1)} %convert_element_type.251), channel_id=1, source_target_pairs={{0,16},{16,0},{1,17},{17,1},{2,18},{18,2},{3,19},{19,3},{4,20},{20... | collective-permute-start | bytes 172040 | tf_op jit(solution)/shard_map/ppermute | solution.py:666
  93.5 1.3 collective-permute-start.18
  93.6 2.0 collective-permute-start.19
  96.0 11.5 %collective-permute-start.25 = (bf16[272,896]{1,0:T(8,128)(2,1)S(1)}, bf16[272,896]{1,0:T(8,128)(2,1)S(1)}, u32[]{:S(2)}, u32[]{:S(2)}) collective-permute-start(bf16[272,896]{1,0:T(8,128)(2,1)S(1)} %fusion.20.refs_8_), channel_id=1, source_target_pairs={{0,4},{5,1},{4,8},{9,5},{8,12},{13,9},{12,14},{15,13},{14,10},{11,... | collective-permute-start | bytes 1462280 | tf_op jit(solution)/shard_map/ppermute | solution.py:81
  97.6 12.4 %collective-permute-start.20 = (bf16[272,896]{1,0:T(8,128)(2,1)S(1)}, bf16[272,896]{1,0:T(8,128)(2,1)S(1)}, u32[]{:S(2)}, u32[]{:S(2)}) collective-permute-start(bf16[272,896]{1,0:T(8,128)(2,1)S(1)} %pad_maximum_fusion.4.refs_4_.refs_0_), channel_id=1, source_target_pairs={{0,4},{5,1},{4,8},{9,5},{8,12},{13,9},{12,14},{15,13},{14,10},{11,... | collective-permute-start | bytes 1462280 | tf_op jit(solution)/shard_map/ppermute | solution.py:81
  107.5 17.0 %copy-start.11 = (bf16[272,896]{1,0:T(8,128)(2,1)}, bf16[272,896]{1,0:T(8,128)(2,1)S(1)}, u32[]{:S(2)}) copy-start(bf16[272,896]{1,0:T(8,128)(2,1)S(1)} %collective-permute-done.25.refs_9_) | copy-start | bytes 1462276
  107.5 8.9 %collective-permute-start.26 = (bf16[272,896]{1,0:T(8,128)(2,1)S(1)}, bf16[272,896]{1,0:T(8,128)(2,1)}, u32[]{:S(2)}, u32[]{:S(2)}) collective-permute-start(bf16[272,896]{1,0:T(8,128)(2,1)S(1)} %collective-permute-done.25.refs_9_), channel_id=1, source_target_pairs={{0,4},{5,1},{4,8},{9,5},{8,12},{13,9},{12,14},{15,13},{14,10},{11,... | collective-permute-start | bytes 1462280 | tf_op jit(solution)/shard_map/ppermute | solution.py:81
  109.0 7.4 %collective-permute-start.27 = (bf16[272,896]{1,0:T(8,128)(2,1)S(1)}, bf16[272,896]{1,0:T(8,128)(2,1)S(1)}, u32[]{:S(2)}, u32[]{:S(2)}) collective-permute-start(bf16[272,896]{1,0:T(8,128)(2,1)S(1)} %collective-permute-done.25.refs_9_), channel_id=1, source_target_pairs={{0,1},{1,0},{2,3},{3,2},{4,5},{5,4},{6,7},{7,6},{8,9},{9,8},{10,11... | collective-permute-start | bytes 1462280 | tf_op jit(solution)/shard_map/ppermute | solution.py:85
  110.1 14.5 %copy-start.12 = (bf16[272,896]{1,0:T(8,128)(2,1)}, bf16[272,896]{1,0:T(8,128)(2,1)S(1)}, u32[]{:S(2)}) copy-start(bf16[272,896]{1,0:T(8,128)(2,1)S(1)} %collective-permute-done.20.refs_5_.refs_1_) | copy-start | bytes 1462276
  110.1 11.5 %collective-permute-start.21 = (bf16[272,896]{1,0:T(8,128)(2,1)S(1)}, bf16[272,896]{1,0:T(8,128)(2,1)S(1)}, u32[]{:S(2)}, u32[]{:S(2)}) collective-permute-start(bf16[272,896]{1,0:T(8,128)(2,1)S(1)} %collective-permute-done.20.refs_5_.refs_1_), channel_id=1, source_target_pairs={{0,4},{5,1},{4,8},{9,5},{8,12},{13,9},{12,14},{15,13},{14,10},{11,... | collective-permute-start | bytes 1462280 | tf_op jit(solution)/shard_map/ppermute | solution.py:81
  111.6 10.0 %collective-permute-start.22 = (bf16[272,896]{1,0:T(8,128)(2,1)S(1)}, bf16[272,896]{1,0:T(8,128)(2,1)S(1)}, u32[]{:S(2)}, u32[]{:S(2)}) collective-permute-start(bf16[272,896]{1,0:T(8,128)(2,1)S(1)} %collective-permute-done.20.refs_5_.refs_1_), channel_id=1, source_target_pairs={{0,1},{1,0},{2,3},{3,2},{4,5},{5,4},{6,7},{7,6},{8,9},{9,8},{10,11... | collective-permute-start | bytes 1462280 | tf_op jit(solution)/shard_map/ppermute | solution.py:85
  116.4 8.1 %copy-start.13 = (bf16[272,896]{1,0:T(8,128)(2,1)}, bf16[272,896]{1,0:T(8,128)(2,1)S(1)}, u32[]{:S(2)}) copy-start(bf16[272,896]{1,0:T(8,128)(2,1)S(1)} %collective-permute-done.27.refs_10_) | copy-start | bytes 1462276
  121.6 12.3 %collective-permute-start.28 = (bf16[272,896]{1,0:T(8,128)(2,1)}, bf16[272,896]{1,0:T(8,128)(2,1)S(1)}, u32[]{:S(2)}, u32[]{:S(2)}) collective-permute-start(bf16[272,896]{1,0:T(8,128)(2,1)} %collective-permute-done.26.refs_11_), channel_id=1, source_target_pairs={{0,4},{5,1},{4,8},{9,5},{8,12},{13,9},{12,14},{15,13},{14,10},{11,... | collective-permute-start | bytes 1462280 | tf_op jit(solution)/shard_map/ppermute | solution.py:81
  123.1 12.7 %collective-permute-start.24 = (bf16[272,896]{1,0:T(8,128)(2,1)S(1)}, bf16[272,896]{1,0:T(8,128)(2,1)S(1)}, u32[]{:S(2)}, u32[]{:S(2)}) collective-permute-start(bf16[272,896]{1,0:T(8,128)(2,1)S(1)} %collective-permute-done.21.refs_7_.refs_3_), channel_id=1, source_target_pairs={{0,4},{5,1},{4,8},{9,5},{8,12},{13,9},{12,14},{15,13},{14,10},{11,... | collective-permute-start | bytes 1462280 | tf_op jit(solution)/shard_map/ppermute | solution.py:81
  133.9 15.8 %copy-start.6 = (bf16[272,896]{1,0:T(8,128)(2,1)}, bf16[272,896]{1,0:T(8,128)(2,1)S(1)}, u32[]{:S(2)}) copy-start(bf16[272,896]{1,0:T(8,128)(2,1)S(1)} %collective-permute-done.28.refs_9_.refs_13_) | copy-start | bytes 1462276
  135.8 13.3 %copy-start.7 = (bf16[272,896]{1,0:T(8,128)(2,1)}, bf16[272,896]{1,0:T(8,128)(2,1)S(1)}, u32[]{:S(2)}) copy-start(bf16[272,896]{1,0:T(8,128)(2,1)S(1)} %collective-permute-done.24.refs_5_) | copy-start | bytes 1462276
  135.9 8.8 %collective-permute-start.30 = (bf16[272,896]{1,0:T(8,128)(2,1)S(1)}, bf16[272,896]{1,0:T(8,128)(2,1)S(1)}, u32[]{:S(2)}, u32[]{:S(2)}) collective-permute-start(bf16[272,896]{1,0:T(8,128)(2,1)S(1)} %broadcast_select_fusion.9), channel_id=1, source_target_pairs={{0,4},{5,1},{4,8},{9,5},{8,12},{13,9},{12,14},{15,13},{14,10},{11,... | collective-permute-start | bytes 1462280 | tf_op jit(solution)/shard_map/ppermute | solution.py:81
  144.7 2.0 collective-permute-start.31
  144.8 3.4 %collective-permute-start.23 = (bf16[272,896]{1,0:T(8,128)(2,1)}, bf16[272,896]{1,0:T(8,128)(2,1)S(1)}, u32[]{:S(2)}, u32[]{:S(2)}) collective-permute-start(bf16[272,896]{1,0:T(8,128)(2,1)} %copy-done.14), channel_id=1, source_target_pairs={{0,1},{1,0},{2,3},{3,2},{4,5},{5,4},{6,7},{7,6},{8,9},{9,8},{10,11... | collective-permute-start | bytes 1462280 | tf_op jit(solution)/shard_map/ppermute | solution.py:85
  145.3 2.8 %collective-permute-start.29 = (bf16[272,896]{1,0:T(8,128)(2,1)S(1)}, bf16[272,896]{1,0:T(8,128)(2,1)S(1)}, u32[]{:S(2)}, u32[]{:S(2)}) collective-permute-start(bf16[272,896]{1,0:T(8,128)(2,1)S(1)} %collective-permute-done.24.refs_5_), channel_id=1, source_target_pairs={{0,1},{1,0},{2,3},{3,2},{4,5},{5,4},{6,7},{7,6},{8,9},{9,8},{10,11... | collective-permute-start | bytes 1462280 | tf_op jit(solution)/shard_map/ppermute | solution.py:85
  145.6 4.1 %collective-permute-start.32 = (bf16[272,896]{1,0:T(8,128)(2,1)}, bf16[272,896]{1,0:T(8,128)(2,1)}, u32[]{:S(2)}, u32[]{:S(2)}) collective-permute-start(bf16[272,896]{1,0:T(8,128)(2,1)} %collective-permute-done.26.refs_11_), channel_id=1, source_target_pairs={{0,1},{1,0},{2,3},{3,2},{4,5},{5,4},{6,7},{7,6},{8,9},{9,8},{10,11... | collective-permute-start | bytes 1462280 | tf_op jit(solution)/shard_map/ppermute | solution.py:85
  146.1 3.6 %collective-permute-start.33 = (bf16[272,896]{1,0:T(8,128)(2,1)S(1)}, bf16[272,896]{1,0:T(8,128)(2,1)}, u32[]{:S(2)}, u32[]{:S(2)}) collective-permute-start(bf16[272,896]{1,0:T(8,128)(2,1)S(1)} %collective-permute-done.28.refs_9_.refs_13_), channel_id=1, source_target_pairs={{0,1},{1,0},{2,3},{3,2},{4,5},{5,4},{6,7},{7,6},{8,9},{9,8},{10,11... | collective-permute-start | bytes 1462280 | tf_op jit(solution)/shard_map/ppermute | solution.py:85
  167.7 13.8 %copy-start.18 = (bf16[96,7168]{1,0:T(8,128)(2,1)S(1)}, bf16[96,7168]{1,0:T(8,128)(2,1)}, u32[]{:S(2)}) copy-start(bf16[96,7168]{1,0:T(8,128)(2,1)} %get-tuple-element.112) | copy-start | bytes 4128772
  167.7 3.5 %collective-permute-start.35 = (bf16[96,7168]{1,0:T(8,128)(2,1)}, bf16[96,7168]{1,0:T(8,128)(2,1)}, u32[]{:S(2)}, u32[]{:S(2)}) collective-permute-start(bf16[96,7168]{1,0:T(8,128)(2,1)} %get-tuple-element.113), channel_id=1, source_target_pairs={{0,1},{1,0},{2,3},{3,2},{4,5},{5,4},{6,7},{7,6},{8,9},{9,8},{10,11... | collective-permute-start | bytes 4128776 | tf_op jit(solution)/shard_map/ppermute | solution.py:85
  172.6 6.3 %collective-permute-start.36 = (bf16[32,3584]{1,0:T(8,128)(2,1)S(1)}, bf16[32,3584]{1,0:T(8,128)(2,1)S(1)}, u32[]{:S(2)}, u32[]{:S(2)}) collective-permute-start(bf16[32,3584]{1,0:T(8,128)(2,1)S(1)} %get-tuple-element.144), channel_id=1, source_target_pairs={{0,4},{5,1},{4,8},{9,5},{8,12},{13,9},{12,14},{15,13},{14,10},{11,... | collective-permute-start | bytes 688136 | tf_op jit(solution)/shard_map/ppermute | solution.py:81
  174.3 7.1 %collective-permute-start.37 = (bf16[32,3584]{1,0:T(8,128)(2,1)S(1)}, bf16[32,3584]{1,0:T(8,128)(2,1)S(1)}, u32[]{:S(2)}, u32[]{:S(2)}) collective-permute-start(bf16[32,3584]{1,0:T(8,128)(2,1)S(1)} %get-tuple-element.143), channel_id=1, source_target_pairs={{0,4},{5,1},{4,8},{9,5},{8,12},{13,9},{12,14},{15,13},{14,10},{11,... | collective-permute-start | bytes 688136 | tf_op jit(solution)/shard_map/ppermute | solution.py:81
  175.8 15.4 %collective-permute-start.34 = (bf16[160,7168]{1,0:T(8,128)(2,1)}, bf16[160,7168]{1,0:T(8,128)(2,1)S(1)}, u32[]{:S(2)}, u32[]{:S(2)}) collective-permute-start(bf16[160,7168]{1,0:T(8,128)(2,1)} %get-tuple-element.111), channel_id=1, source_target_pairs={{0,1},{1,0},{2,3},{3,2},{4,5},{5,4},{6,7},{7,6},{8,9},{9,8},{10,11... | collective-permute-start | bytes 6881288 | tf_op jit(solution)/shard_map/ppermute | solution.py:85
  182.7 8.5 %collective-permute-start.39 = (bf16[64,3584]{1,0:T(8,128)(2,1)S(1)}, bf16[64,3584]{1,0:T(8,128)(2,1)S(1)}, u32[]{:S(2)}, u32[]{:S(2)}) collective-permute-start(bf16[64,3584]{1,0:T(8,128)(2,1)S(1)} %add_convert_fusion.6), channel_id=1, source_target_pairs={{0,4},{5,1},{4,8},{9,5},{8,12},{13,9},{12,14},{15,13},{14,10},{11,... | collective-permute-start | bytes 1376264 | tf_op jit(solution)/shard_map/ppermute | solution.py:81
  185.4 10.8 %collective-permute-start.38 = (bf16[64,3584]{1,0:T(8,128)(2,1)S(1)}, bf16[64,3584]{1,0:T(8,128)(2,1)S(1)}, u32[]{:S(2)}, u32[]{:S(2)}) collective-permute-start(bf16[64,3584]{1,0:T(8,128)(2,1)S(1)} %add_convert_fusion.5), channel_id=1, source_target_pairs={{0,4},{5,1},{4,8},{9,5},{8,12},{13,9},{12,14},{15,13},{14,10},{11,... | collective-permute-start | bytes 1376264 | tf_op jit(solution)/shard_map/ppermute | solution.py:81
  191.4 9.6 %collective-permute-start.41 = (bf16[64,3584]{1,0:T(8,128)(2,1)S(1)}, bf16[64,3584]{1,0:T(8,128)(2,1)S(1)}, u32[]{:S(2)}, u32[]{:S(2)}) collective-permute-start(bf16[64,3584]{1,0:T(8,128)(2,1)S(1)} %add_convert_fusion.4), channel_id=1, source_target_pairs={{0,4},{5,1},{4,8},{9,5},{8,12},{13,9},{12,14},{15,13},{14,10},{11,... | collective-permute-start | bytes 1376264 | tf_op jit(solution)/shard_map/ppermute | solution.py:81
  196.3 9.7 %collective-permute-start.40 = (bf16[64,3584]{1,0:T(8,128)(2,1)S(1)}, bf16[64,3584]{1,0:T(8,128)(2,1)S(1)}, u32[]{:S(2)}, u32[]{:S(2)}) collective-permute-start(bf16[64,3584]{1,0:T(8,128)(2,1)S(1)} %add_convert_fusion.3), channel_id=1, source_target_pairs={{0,4},{5,1},{4,8},{9,5},{8,12},{13,9},{12,14},{15,13},{14,10},{11,... | collective-permute-start | bytes 1376264 | tf_op jit(solution)/shard_map/ppermute | solution.py:81
  201.2 9.6 %collective-permute-start.42 = (bf16[64,3584]{1,0:T(8,128)(2,1)S(1)}, bf16[64,3584]{1,0:T(8,128)(2,1)S(1)}, u32[]{:S(2)}, u32[]{:S(2)}) collective-permute-start(bf16[64,3584]{1,0:T(8,128)(2,1)S(1)} %add_convert_fusion.2), channel_id=1, source_target_pairs={{0,4},{5,1},{4,8},{9,5},{8,12},{13,9},{12,14},{15,13},{14,10},{11,... | collective-permute-start | bytes 1376264 | tf_op jit(solution)/shard_map/ppermute | solution.py:81
  206.0 16.8 %copy-start.1 = (bf16[32,64,576]{2,1,0:T(8,128)(2,1)S(1)}, bf16[32,64,576]{2,1,0:T(8,128)(2,1)}, u32[]{:S(2)}) copy-start(bf16[32,64,576]{2,1,0:T(8,128)(2,1)} %param.13) | copy-start | bytes 7077892
  210.9 1.6 collective-permute-start.43
  211.0 8.5 %collective-permute-start.45 = (bf16[64,3584]{1,0:T(8,128)(2,1)S(1)}, bf16[64,3584]{1,0:T(8,128)(2,1)S(1)}, u32[]{:S(2)}, u32[]{:S(2)}) collective-permute-start(bf16[64,3584]{1,0:T(8,128)(2,1)S(1)} %add_convert_fusion.1), channel_id=1, source_target_pairs={{0,4},{5,1},{4,8},{9,5},{8,12},{13,9},{12,14},{15,13},{14,10},{11,... | collective-permute-start | bytes 1376264 | tf_op jit(solution)/shard_map/ppermute | solution.py:81
  212.6 7.7 %collective-permute-start.44 = (bf16[32,3584]{1,0:T(8,128)(2,1)S(1)}, bf16[32,3584]{1,0:T(8,128)(2,1)S(1)}, u32[]{:S(2)}, u32[]{:S(2)}) collective-permute-start(bf16[32,3584]{1,0:T(8,128)(2,1)S(1)} %add_convert_fusion.8), channel_id=1, source_target_pairs={{0,16},{16,0},{1,17},{17,1},{2,18},{18,2},{3,19},{19,3},{4,20},{20... | collective-permute-start | bytes 688136 | tf_op jit(solution)/shard_map/ppermute | solution.py:185
  220.4 1.6 collective-permute-start.46
  (17 other events, 47.4 us)
